TPU v7x, 512 devices: a whole 4x4x16 slice. The times are simulated.
512 devices in a mesh: seq: 128 (over x_lo, z, y), head: 4 (over x_hi, core).
Axes of the slice: x: 4 (x_hi: 2, x_lo: 2; x = x_hi * 2 + x_lo), y: 4, z: 16, core: 2. Of those that a mesh axis runs over, the one named last changes fastest.
Arguments:
- queries: bfloat16 [16384, 8192], P(('seq', 'head')), may hold values from -5 to 5
- output_gradient: bfloat16 [16384, 8192], P(('seq', 'head')), may hold values from -5 to 5
- response_key_value: bfloat16 [16384, 2, 1024], P(('seq', 'head')), may hold values from -5 to 5
- prompt_key_value: bfloat16 [2048, 2, 1024], P('seq', None, 'head'), may hold values from -5 to 5
- packing: int32 [128], replicated, may hold values from 0 to 127, each once
- lengths: int32 [128], replicated, may hold values from 1 to 128, as said below
- prompt_owner: int32 [128], replicated, may hold values from 0 to 127, each once
Outputs:
- query_grad: bfloat16 [16384, 8192], P(('seq', 'head'))
- resp_grad: bfloat16 [16384, 2, 1024], P(('seq', 'head'))
- prompt_grad: float32 [2048, 2, 1024], P('seq', None, 'head')
Inputs may be any that keep to these rules, and one draw needn't show every extreme that they name: `packing`: every response is held by exactly one index of seq. `prompt_owner`: every index of seq holds exactly one prompt piece. `lengths`: some response fills all 128 slots.
All inputs are finite; a program needn't handle non-finite values.
Results may differ from a plain program's by a relative error of at most 0.0094.
Values may be sent and summed in bfloat16 or wider, within the bound.
No kernel may reach another device: no remote copies, remote signals or barrier semaphores. Data moves between devices by JAX's collectives and lax.ppermute only.
A program may use at most 64 MiB of HBM per device.

v0:
```python
import math

import jax
import jax.numpy as jnp
from jax import lax
from jax.sharding import PartitionSpec as P

QUERY_HEADS = 64
KEY_VALUE_HEADS = 8
HEAD_SIZE = 128


def block_grads(query_block, grad_block, key_rows, value_rows, length, prompt_len, inv_root):
    row_count = query_block.shape[0]
    scores = (
        jnp.einsum("ird,kd->irk", query_block, key_rows, preferred_element_type=jnp.float32)
        * inv_root
    )
    query_pos = jnp.arange(row_count, dtype=jnp.int32)[:, None, None]
    key_pos = jnp.arange(key_rows.shape[0], dtype=jnp.int32)[None, None, :]
    valid = query_pos < length
    allowed = ((key_pos < prompt_len) | (key_pos - prompt_len <= query_pos)) & valid
    row_max = jnp.max(jnp.where(allowed, scores, -jnp.inf), axis=-1, keepdims=True)
    row_max = jnp.where(valid, row_max, 0.0)
    exponent = jnp.where(allowed, jnp.exp(scores - row_max), 0.0)
    row_total = jnp.sum(exponent, axis=-1, keepdims=True)
    weights = exponent / jnp.where(valid, row_total, 1.0)
    weight_half = weights.astype(jnp.bfloat16)
    outputs = jnp.einsum("irk,kd->ird", weight_half, value_rows, preferred_element_type=jnp.float32)
    delta = jnp.sum(grad_block.astype(jnp.float32) * outputs, axis=-1, keepdims=True)
    dprob = jnp.einsum("ird,kd->irk", grad_block, value_rows, preferred_element_type=jnp.float32)
    dscore_half = (weights * (dprob - delta)).astype(jnp.bfloat16)
    query_grad = (
        jnp.einsum("irk,kd->ird", dscore_half, key_rows, preferred_element_type=jnp.float32)
        * inv_root
    )
    key_gradient = (
        jnp.einsum("irk,ird->kd", dscore_half, query_block, preferred_element_type=jnp.float32)
        * inv_root
    )
    value_gradient = jnp.einsum(
        "irk,ird->kd", weight_half, grad_block, preferred_element_type=jnp.float32
    )
    return (query_grad, key_gradient, value_gradient)


def shards(
    queries, output_gradient, response_key_value, prompt_key_value, packing, lengths, prompt_owner
):
    seq_count = lax.axis_size("seq")
    position = lax.axis_index("seq")
    prompts = max(1, seq_count // 16)
    group_size = seq_count // prompts
    piece_rows = prompt_key_value.shape[0]
    prompt_len = piece_rows * group_size
    grouped_heads = QUERY_HEADS // KEY_VALUE_HEADS
    inv_root = 1.0 / math.sqrt(HEAD_SIZE)
    local_rows = queries.shape[0]
    full_width = queries.shape[1]
    query_complete, grad_all, kv_all = (
        lax.all_to_all(
            queries.reshape(local_rows, 1, full_width),
            "head",
            split_axis=2,
            concat_axis=0,
            tiled=True,
        ),
        lax.all_to_all(
            output_gradient.reshape(local_rows, 1, full_width),
            "head",
            split_axis=2,
            concat_axis=0,
            tiled=True,
        ),
        lax.all_to_all(response_key_value, "head", split_axis=2, concat_axis=0, tiled=True),
    )
    slot_rows = query_complete.shape[0]
    response = packing[position]
    length = lengths[response]
    prompt = response // group_size
    owners = lax.dynamic_slice_in_dim(prompt_owner, prompt * group_size, group_size)
    sender_rows = (
        owners[:, None] * piece_rows + jnp.arange(piece_rows, dtype=jnp.int32)[None, :]
    ).reshape(prompt_len)
    everything = lax.all_gather(prompt_key_value, "seq", axis=0, tiled=True)
    prompt_row_block = jnp.take(everything, sender_rows, axis=0)
    n_groups = kv_all.shape[2] // HEAD_SIZE
    block_rows = min(128, slot_rows)
    key_tally = prompt_len + slot_rows
    query_parts = []
    own_parts = []
    prompt_parts = []
    for group in range(n_groups):
        head_lo = group * grouped_heads * HEAD_SIZE
        head_hi = head_lo + grouped_heads * HEAD_SIZE
        group_queries = query_complete[:, 0, head_lo:head_hi].reshape(
            slot_rows, grouped_heads, HEAD_SIZE
        )
        group_grads = grad_all[:, 0, head_lo:head_hi].reshape(slot_rows, grouped_heads, HEAD_SIZE)
        key_rows = jnp.concatenate(
            [
                prompt_row_block[:, 0, group * HEAD_SIZE : (group + 1) * HEAD_SIZE],
                kv_all[:, 0, group * HEAD_SIZE : (group + 1) * HEAD_SIZE],
            ],
            axis=0,
        )
        value_rows = jnp.concatenate(
            [
                prompt_row_block[:, 1, group * HEAD_SIZE : (group + 1) * HEAD_SIZE],
                kv_all[:, 1, group * HEAD_SIZE : (group + 1) * HEAD_SIZE],
            ],
            axis=0,
        )
        query_block = group_queries
        grad_block = group_grads

        def active():
            return block_grads(
                query_block, grad_block, key_rows, value_rows, length, prompt_len, inv_root
            )

        def skipped():
            return (
                jnp.zeros((block_rows, grouped_heads, HEAD_SIZE), jnp.float32),
                jnp.zeros((key_tally, HEAD_SIZE), jnp.float32),
                jnp.zeros((key_tally, HEAD_SIZE), jnp.float32),
            )

        block_query, block_key, block_value = lax.cond(0 < length, active, skipped)
        query_parts.append(block_query.reshape(slot_rows, grouped_heads * HEAD_SIZE))
        own_parts.append(jnp.stack([block_key[prompt_len:], block_value[prompt_len:]], axis=1))
        prompt_parts.append(jnp.stack([block_key[:prompt_len], block_value[:prompt_len]], axis=1))
    query_grad = jnp.concatenate(query_parts, axis=1).astype(jnp.bfloat16).reshape(slot_rows, 1, -1)
    own_grad = jnp.concatenate(own_parts, axis=2).astype(jnp.bfloat16)
    partial_value = jnp.concatenate(prompt_parts, axis=2)
    query_back, own_back = (
        lax.all_to_all(query_grad, "head", split_axis=0, concat_axis=2, tiled=True),
        lax.all_to_all(own_grad, "head", split_axis=0, concat_axis=2, tiled=True),
    )
    inside = (sender_rows >= 0) & (sender_rows < piece_rows * lax.axis_size("seq"))
    target = jnp.where(inside, sender_rows, piece_rows * lax.axis_size("seq"))
    prompt_out = lax.psum_scatter(
        jnp.zeros((piece_rows * lax.axis_size("seq"), 2, partial_value.shape[2]), jnp.float32)
        .at[target]
        .add(partial_value, mode="drop"),
        "seq",
        scatter_dimension=0,
        tiled=True,
    )
    return (query_back.reshape(local_rows, full_width), own_back, prompt_out)


def solution(mesh):
    return jax.shard_map(
        shards,
        mesh=mesh,
        in_specs=(
            P(("seq", "head"), None),
            P(("seq", "head"), None),
            P(("seq", "head"), None, None),
            P("seq", None, "head"),
            P(),
            P(),
            P(),
        ),
        out_specs=(
            P(("seq", "head"), None),
            P(("seq", "head"), None, None),
            P("seq", None, "head"),
        ),
        check_vma=False,
    )
```

profile of v0, /device:TPU:4, one launch (start us, length us, event | category | flops | bytes accessed | tf_op | source)
XLA Modules:
  0.0 1863.4 jit_solution(2555126971021509110)
XLA Ops:
  7.2 0.7 all-gather.2.cloned.1.call-update
  7.9 1.4 copy.182
  9.3 1.2 reshape.370
  10.5 9.2 all-to-all-start.1
  19.6 0.6 dynamic_slice.9
  22.8 6.7 copy.179
  29.6 0.5 broadcast.295
  30.1 45.2 %reduce = bf16[8192,32]{1,0:T(8,128)(2,1)S(1)} reduce(bf16[8192,1,32]{2,1,0:T(2,128)(2,1)} %bitcast.130, bf16[]{:T(256)} %broadcast.295), dimensions={1}, to_apply=%bitcast.104.reduce_sub_computation | reduce | bytes 1048578
  75.3 2.9 reshape.368
  78.3 5.3 all-to-all-start
  83.8 6.7 copy.185
  90.6 45.2 %reduce.1 = bf16[8192,32]{1,0:T(8,128)(2,1)S(1)} reduce(bf16[8192,1,32]{2,1,0:T(2,128)(2,1)} %bitcast.133, bf16[]{:T(256)} %broadcast.295), dimensions={1}, to_apply=%bitcast.108.reduce_sub_computation | reduce | bytes 1048578
  135.8 3.0 reshape.372
  138.7 4.8 all-to-all-start.2
  144.9 0.6 dynamic_slice.10
  146.4 0.4 copy.222
  146.9 3.3 reshape.369
  150.2 8.0 copy.180
  158.2 0.4 all_to_all.64
  158.9 3.3 reshape.373
  162.2 8.0 copy.186
  170.2 0.4 all_to_all.72
  170.9 432.6 %all-gather.2.cloned.1.call-done = bf16[2048,2,256]{2,1,0:T(2,128)(2,1)} async-done(((bf16[16,2,256]{2,1,0:T(2,128)(2,1)}), bf16[2048,2,256]{2,1,0:T(2,128)(2,1)}) %all-gather.2.cloned.1.call-update) | async-done | bytes 2097168 | tf_op jit(solution)/shard_map/all_gather | solution.py:85
  603.5 2.8 gather_fusion
  606.3 0.9 broadcast_select_fusion.4
  607.3 0.4 fusion.34
  607.8 6.2 conditional.3
  608.3 0.7 iota_compare_fusion.5
  609.3 0.5 select_reduce_fusion.1
  609.9 0.6 fusion.16
  610.5 0.7 fusion.18
  611.2 0.7 multiply_convert_fusion.1
  611.9 0.4 fusion.19
  612.3 0.8 convolution_bitcast_fusion.2
  613.1 0.4 fusion.17
  613.5 0.5 copy.226
  614.1 0.7 pad_maximum_fusion.1
  614.7 6.1 conditional.2
  615.0 0.7 iota_compare_fusion.2
  616.1 0.5 select_reduce_fusion
  616.7 0.6 fusion.1
  617.3 0.7 fusion.3
  617.9 0.7 multiply_convert_fusion
  618.7 0.4 fusion.4
  619.1 0.8 convolution_bitcast_fusion
  619.9 0.4 fusion.2
  620.3 0.5 copy.224
  620.9 0.4 copy.201
  621.3 2.9 broadcast_in_dim.94
  624.1 26.0 %scatter_fusion = f32[2048,2,256]{2,1,0:T(2,128)} fusion(f32[2048,2,256]{2,1,0:T(2,128)} %broadcast_in_dim.94, s32[256]{0:T(256)S(1)} %bitcast.168, f32[256,2,256]{2,1,0:T(2,128)S(1)} %copy.201), kind=kCustom, calls=%fused_computation.1 | custom fusion | flops 131072 | bytes 1573888 | tf_op jit(solution)/shard_map/scatter-add | solution.py:145
  650.3 0.8 copy.199
  651.1 5.0 all-to-all-start.4
  656.1 1.1 pad_maximum_fusion
  657.2 3.7 reduce.2
  660.9 1.2 reshape.374
  662.1 4.8 all-to-all-start.3
  666.9 1.3 dynamic-slice
  668.8 0.7 copy.232
  669.5 4.5 all-to-all-done.3
  674.0 0.5 reshape.375
  674.9 0.4 copy.198
  675.3 1.1 copy.233
  676.4 1178.6 %all-reduce.3.cloned.1.call-done = f32[2048,2,256]{2,1,0:T(2,128)} async-done(((f32[2048,2,256]{2,1,0:T(2,128)}), f32[2048,2,256]{2,1,0:T(2,128)}) %all-reduce.3.cloned.1.call-update) | async-done | bytes 4194320
  1855.0 1.4 constant_dynamic-slice_fusion
  (65 shorter events, 3.2 us)
Async XLA Ops:
  7.2 12.5 copy-start.3
  7.2 15.7 copy-start
  7.2 596.3 %all-gather.2.cloned.1.call-start = ((), (), s32[]{:S(2)}) async-start(), calls=%async_computation.5 | async-start | bytes 2113536 | tf_op jit(solution)/shard_map/all_gather | solution.py:85
  10.5 67.9 %all-to-all-start.1 = ((bf16[4,2,8192]{2,1,0:T(2,128)(2,1)}), bf16[4,2,8192]{2,1,0:T(2,128)(2,1)S(1)}, u32[]{:S(2)}, u32[]{:S(2)}) async-start(bf16[4,2,8192]{2,1,0:T(2,128)(2,1)} %reshape.370), calls=%async_computation.1 | async-start | bytes 262144 | tf_op jit(solution)/shard_map/all_to_all | solution.py:75
  75.3 3.0 copy-start.4
  75.3 8.5 copy-start.1
  78.3 60.4 %all-to-all-start = ((bf16[4,2,32768]{2,1,0:T(2,128)(2,1)}), bf16[4,2,32768]{2,1,0:T(2,128)(2,1)S(1)}, u32[]{:S(2)}, u32[]{:S(2)}) async-start(bf16[4,2,32768]{2,1,0:T(2,128)(2,1)} %reshape.368), calls=%async_computation | async-start | bytes 1048576 | tf_op jit(solution)/shard_map/all_to_all | solution.py:61
  135.8 9.1 copy-start.5
  138.7 20.1 %all-to-all-start.2 = ((bf16[4,2,32768]{2,1,0:T(2,128)(2,1)}), bf16[4,2,32768]{2,1,0:T(2,128)(2,1)S(1)}, u32[]{:S(2)}, u32[]{:S(2)}) async-start(bf16[4,2,32768]{2,1,0:T(2,128)(2,1)} %reshape.372), calls=%async_computation.2 | async-start | bytes 1048576 | tf_op jit(solution)/shard_map/all_to_all | solution.py:68
  143.6 1711.4 %all-reduce.3.cloned.1.call-start = ((), (), s32[]{:S(2)}) async-start(), calls=%async_computation.6 | async-start | bytes 8388608
  616.1 1.1 copy-start.2
  651.1 11.0 all-to-all-start.4
  662.1 12.0 all-to-all-start.3
Sparse Core Ops, SparseCore 0:
  10.1 593.3 all-gather.1
  650.3 1204.6 all-reduce.2
where the time goes:
time: 1870 us; the launch traced here: 1860 us
  waiting for transfers between devices  1620 us (87%)
  other arithmetic  126 us (7%)
  local copies, waits for them, and re-layouts  64.8 us (3%)
  starting transfers between devices  29.1 us (2%)
  between operations  19.9 us (1%)
    unnamed x3, waiting for transfers between devices  1180 us
    all_gather x1, waiting for transfers between devices, shards(): everything = lax.all_gather(prompt_key_value, 'seq', axis=0, tiled=True)  433 us
    unnamed x2, other arithmetic  90.4 us
  transfers between devices with their start and end apart: 7, of which 3 were waited for; matrix products, arithmetic and copies ran while one was open for 8% of the time, Pallas kernels for 0%

commit v1 on v0

v1 whole, which is shorter than its diff:
```python
import math

import jax
import jax.numpy as jnp
from jax import lax
from jax.experimental import pallas as pl
from jax.experimental.pallas import tpu as pltpu
from jax.sharding import Mesh
from jax.sharding import PartitionSpec as P

QUERY_HEADS = 64
KEY_VALUE_HEADS = 8
HEAD = 128
GROUP = 16
PIECE = 16
PROMPT = GROUP * PIECE
SLOTS = 128
KEYS = PROMPT + SLOTS
X_LO, Z, Y = 2, 16, 4
PLANE = X_LO * Y
N_SEQ = PLANE * Z
N_HEAD = 4
LOCAL_ROWS = SLOTS // N_HEAD
KV_LOCAL = KEY_VALUE_HEADS // N_HEAD
PER_GROUP = QUERY_HEADS // KEY_VALUE_HEADS
Q_WIDTH = KV_LOCAL * PER_GROUP * HEAD
KV_WIDTH = KV_LOCAL * HEAD
IN_WIDTH = 2 * Q_WIDTH + 2 * KV_WIDTH
OUT_WIDTH = Q_WIDTH + 2 * KV_WIDTH
INV_ROOT = 1.0 / math.sqrt(HEAD)
EXP2_SCALE = INV_ROOT / math.log(2.0)

BF16 = jnp.bfloat16
F32 = jnp.float32
SMEM = pl.BlockSpec(memory_space=pltpu.SMEM)
VMEM = pl.BlockSpec(memory_space=pltpu.VMEM)


def params(mib):
    return pltpu.CompilerParams(vmem_limit_bytes=mib * 2**20)


def dot(a, b, contract):
    return lax.dot_general(a, b, (contract, ((), ())), preferred_element_type=F32)


def spread_kernel(piece_ref, out_ref):
    flat = jnp.concatenate([piece_ref[:, 0, :], piece_ref[:, 1, :]], axis=1)
    for z in range(Z):
        out_ref[z] = flat


def spread_piece(piece):
    return pl.pallas_call(
        spread_kernel,
        out_shape=jax.ShapeDtypeStruct((Z, PIECE, 2 * KV_WIDTH), BF16),
        in_specs=[VMEM],
        out_specs=VMEM,
        compiler_params=params(16),
    )(piece)


def pack_kernel(q_ref, g_ref, kv_ref, out_ref):
    out_ref[0, :, :Q_WIDTH] = q_ref[...]
    out_ref[0, :, Q_WIDTH : 2 * Q_WIDTH] = g_ref[...]
    out_ref[0, :, 2 * Q_WIDTH : 2 * Q_WIDTH + KV_WIDTH] = kv_ref[:, 0, :]
    out_ref[0, :, 2 * Q_WIDTH + KV_WIDTH :] = kv_ref[:, 1, :]


def pack_rows(queries, grads, kv):
    return pl.pallas_call(
        pack_kernel,
        grid=(N_HEAD,),
        out_shape=jax.ShapeDtypeStruct((N_HEAD, LOCAL_ROWS, IN_WIDTH), BF16),
        in_specs=[
            pl.BlockSpec((LOCAL_ROWS, Q_WIDTH), lambda h: (0, h)),
            pl.BlockSpec((LOCAL_ROWS, Q_WIDTH), lambda h: (0, h)),
            pl.BlockSpec((LOCAL_ROWS, 2, KV_WIDTH), lambda h: (0, 0, h)),
        ],
        out_specs=pl.BlockSpec((1, LOCAL_ROWS, IN_WIDTH), lambda h: (h, 0, 0)),
        compiler_params=params(16),
    )(queries, grads, kv)


def unpack_kernel(in_ref, q_ref, kv_ref):
    q_ref[...] = in_ref[0, :, :Q_WIDTH]
    kv_ref[:, 0, :] = in_ref[0, :, Q_WIDTH : Q_WIDTH + KV_WIDTH]
    kv_ref[:, 1, :] = in_ref[0, :, Q_WIDTH + KV_WIDTH :]


def unpack_rows(back):
    return pl.pallas_call(
        unpack_kernel,
        grid=(N_HEAD,),
        out_shape=(
            jax.ShapeDtypeStruct((LOCAL_ROWS, N_HEAD * Q_WIDTH), BF16),
            jax.ShapeDtypeStruct((LOCAL_ROWS, 2, N_HEAD * KV_WIDTH), BF16),
        ),
        in_specs=[pl.BlockSpec((1, LOCAL_ROWS, OUT_WIDTH), lambda h: (h, 0, 0))],
        out_specs=(
            pl.BlockSpec((LOCAL_ROWS, Q_WIDTH), lambda h: (0, h)),
            pl.BlockSpec((LOCAL_ROWS, 2, KV_WIDTH), lambda h: (0, 0, h)),
        ),
        compiler_params=params(16),
    )(back)


def sum_plane_kernel(in_ref, out_ref):
    total = in_ref[0].astype(F32)
    for i in range(1, PLANE):
        total += in_ref[i].astype(F32)
    out_ref[...] = total.astype(BF16)


def sum_plane(parts):
    return pl.pallas_call(
        sum_plane_kernel,
        out_shape=jax.ShapeDtypeStruct((Z * PIECE, 2 * KV_WIDTH), BF16),
        in_specs=[VMEM],
        out_specs=VMEM,
        compiler_params=params(16),
    )(parts)


def sum_line_kernel(in_ref, out_ref):
    total = in_ref[0].astype(F32)
    for i in range(1, Z):
        total += in_ref[i].astype(F32)
    out_ref[:, 0, :] = total[:, :KV_WIDTH]
    out_ref[:, 1, :] = total[:, KV_WIDTH:]


def sum_line(parts):
    return pl.pallas_call(
        sum_line_kernel,
        out_shape=jax.ShapeDtypeStruct((PIECE, 2, KV_WIDTH), F32),
        in_specs=[VMEM],
        out_specs=VMEM,
        compiler_params=params(16),
    )(parts)


def rows_of(ref, lo):
    return ref[:, :, lo : lo + HEAD].reshape(SLOTS, HEAD)


def attention_kernel(
    pos_ref, packing_ref, lengths_ref, owner_ref, rows_ref, pieces_ref,
    back_ref, grads_ref, key_ref, value_ref, weight_ref, dscore_ref,
):
    response = packing_ref[pos_ref[0]]
    length = lengths_ref[response]
    first = (response // GROUP) * GROUP
    places = []
    for j in range(GROUP):
        s = owner_ref[first + j]
        places.append(((s // (Z * Y)) * Y + s % Y) * Z + (s // Y) % Z)
    for j in range(GROUP):
        piece = pieces_ref[places[j]]
        key_ref[j * PIECE : (j + 1) * PIECE, :] = piece[:, :KV_WIDTH]
        value_ref[j * PIECE : (j + 1) * PIECE, :] = piece[:, KV_WIDTH:]
    for g in range(KV_LOCAL):
        cols = slice(g * HEAD, (g + 1) * HEAD)
        key_ref[PROMPT:, cols] = rows_of(rows_ref, 2 * Q_WIDTH + g * HEAD)
        value_ref[PROMPT:, cols] = rows_of(rows_ref, 2 * Q_WIDTH + KV_WIDTH + g * HEAD)
    grads_ref[...] = jnp.zeros_like(grads_ref)

    pair = 2
    width = pair * SLOTS
    query_pos = lax.broadcasted_iota(jnp.int32, (SLOTS, width), 1) % SLOTS
    causal = lax.broadcasted_iota(jnp.int32, (SLOTS, width), 0) <= query_pos
    used = query_pos[:1] < length

    for g in range(KV_LOCAL):
        cols = slice(g * HEAD, (g + 1) * HEAD)
        keys, values = key_ref[:, cols], value_ref[:, cols]
        queries, out_grads = [], []
        for c in range(PER_GROUP // pair):
            at = [(g * PER_GROUP + c * pair + i) * HEAD for i in range(pair)]
            query = jnp.concatenate([rows_of(rows_ref, lo) for lo in at], axis=0)
            out_grad = jnp.concatenate([rows_of(rows_ref, Q_WIDTH + lo) for lo in at], axis=0)
            queries.append(query)
            out_grads.append(out_grad)
            score = dot(keys, query, ((1,), (1,)))
            score = jnp.concatenate(
                [score[:PROMPT], jnp.where(causal, score[PROMPT:], -jnp.inf)], axis=0
            )
            top = jnp.max(score, axis=0, keepdims=True)
            raised = jnp.exp2((score - top) * EXP2_SCALE)
            total = jnp.sum(raised, axis=0, keepdims=True)
            weight = raised * jnp.where(used, 1.0 / total, 0.0)
            weight_half = weight.astype(BF16)
            dprob = dot(values, out_grad, ((1,), (1,)))
            delta = jnp.sum(weight_half.astype(F32) * dprob, axis=0, keepdims=True)
            dscore = (weight * (dprob - delta)).astype(BF16)
            weight_ref[:, c * width : (c + 1) * width] = weight_half
            dscore_ref[:, c * width : (c + 1) * width] = dscore
            query_grad = dot(keys, dscore, ((0,), (0,))).T * INV_ROOT
            for i, lo in enumerate(at):
                block = query_grad[i * SLOTS : (i + 1) * SLOTS].astype(BF16)
                back_ref[:, :, lo : lo + HEAD] = block.reshape(N_HEAD, LOCAL_ROWS, HEAD)
        key_grad = dot(dscore_ref[...], jnp.concatenate(queries, axis=0), ((1,), (0,))) * INV_ROOT
        value_grad = dot(weight_ref[...], jnp.concatenate(out_grads, axis=0), ((1,), (0,)))
        for slot, grad in enumerate((key_grad, value_grad)):
            grad = grad.astype(BF16)
            lo = slot * KV_WIDTH + g * HEAD
            for j in range(GROUP):
                grads_ref[places[j], :, lo : lo + HEAD] = grad[j * PIECE : (j + 1) * PIECE]
            back_ref[:, :, Q_WIDTH + lo : Q_WIDTH + lo + HEAD] = grad[PROMPT:].reshape(
                N_HEAD, LOCAL_ROWS, HEAD
            )


def attention(pos, packing, lengths, owner, rows, pieces):
    flops = 2 * 5 * KEYS * Q_WIDTH // HEAD * SLOTS * HEAD
    return pl.pallas_call(
        attention_kernel,
        out_shape=(
            jax.ShapeDtypeStruct((N_HEAD, LOCAL_ROWS, OUT_WIDTH), BF16),
            jax.ShapeDtypeStruct((N_SEQ, PIECE, 2 * KV_WIDTH), BF16),
        ),
        in_specs=[SMEM, SMEM, SMEM, SMEM, VMEM, VMEM],
        out_specs=(VMEM, VMEM),
        scratch_shapes=[
            pltpu.VMEM((KEYS, KV_WIDTH), BF16),
            pltpu.VMEM((KEYS, KV_WIDTH), BF16),
            pltpu.VMEM((KEYS, PER_GROUP * SLOTS), BF16),
            pltpu.VMEM((KEYS, PER_GROUP * SLOTS), BF16),
        ],
        compiler_params=params(32),
        cost_estimate=pl.CostEstimate(
            flops=flops, bytes_accessed=6 * 2**20, transcendentals=KEYS * SLOTS * 16
        ),
    )(pos, packing, lengths, owner, rows, pieces)


def exchange(parts, axes):
    return lax.all_to_all(parts, axes, split_axis=0, concat_axis=0, tiled=True)


def shards(queries, out_grads, response_kv, prompt_kv, packing, lengths, owner):
    position = lax.axis_index(("xl", "z", "y")).astype(jnp.int32).reshape(1)
    line = exchange(spread_piece(prompt_kv), "z")
    line = line.reshape(Z * PIECE, 2 * KV_WIDTH)
    pieces = exchange(jnp.broadcast_to(line[None], (PLANE,) + line.shape), ("xl", "y"))
    rows = exchange(pack_rows(queries, out_grads, response_kv), ("xh", "c"))
    back, grads = attention(
        position, packing, lengths, owner, rows, pieces.reshape(N_SEQ, PIECE, 2 * KV_WIDTH)
    )
    grads = exchange(grads.reshape(PLANE, Z * PIECE, 2 * KV_WIDTH), ("xl", "y"))
    grads = exchange(sum_plane(grads).reshape(Z, PIECE, 2 * KV_WIDTH), "z")
    query_grad, resp_grad = unpack_rows(exchange(back, ("xh", "c")))
    return query_grad, resp_grad, sum_line(grads)


def solution(mesh):
    fine = Mesh(mesh.devices.reshape(X_LO, Z, Y, 2, 2), ("xl", "z", "y", "xh", "c"))
    seq, head = ("xl", "z", "y"), ("xh", "c")
    return jax.shard_map(
        shards,
        mesh=fine,
        in_specs=(
            P(seq + head, None),
            P(seq + head, None),
            P(seq + head, None, None),
            P(seq, None, head),
            P(),
            P(),
            P(),
        ),
        out_specs=(
            P(seq + head, None),
            P(seq + head, None, None),
            P(seq, None, head),
        ),
        check_vma=False,
    )
```

time: 1870 us -> 168 us (0.09)
  the two profiles are of different devices: /device:TPU:4 before, /device:TPU:64 now
where the time goes in v1:
time: 168 us; the launch traced here: 167 us
  waiting for transfers between devices  67.1 us (40%)
  blocking collectives  63.2 us (38%)
  starting transfers between devices  22.2 us (13%)
  Pallas kernels  9.69 us (6%)
  local copies, waits for them, and re-layouts  4.52 us (3%)
    all_to_all x4, waiting for transfers between devices, exchange(): return lax.all_to_all(parts, axes, split_axis=0, concat_axis=0, tiled=True)  67.1 us
    all_to_all x2, blocking collectives, exchange(): return lax.all_to_all(parts, axes, split_axis=0, concat_axis=0, tiled=True)  63.2 us
    all_to_all x4, starting transfers between devices, exchange(): return lax.all_to_all(parts, axes, split_axis=0, concat_axis=0, tiled=True)  22.2 us
    pallas_call x1, Pallas kernels, attention(): pl.pallas_call(attention_kernel, out_shape=(jax.ShapeDtypeStruct((N_HEAD,...  4.77 us
  transfers between devices with their start and end apart: 4, of which 4 were waited for; matrix products, arithmetic and copies ran while one was open for 0% of the time, Pallas kernels for 1%

profile of v1, /device:TPU:64, one launch (start us, length us, event | category | flops | bytes accessed | tf_op | source)
XLA Modules:
  0.0 167.4 jit_solution(15944634157358170189)
XLA Ops:
  0.6 0.0 copy-start.1
  0.6 1.0 copy-done.1
  1.7 0.0 copy-start.2
  1.7 1.0 copy-done.2
  2.7 0.0 copy-start.3
  2.7 0.9 copy-done.3
  3.6 0.0 copy-start.4
  3.6 1.8 %shard_map.94 = bf16[4,32,4608]{2,1,0:T(8,128)(2,1)} custom-call(bf16[32,8192]{1,0:T(8,128)(2,1)S(1)} %copy-done.1, bf16[32,8192]{1,0:T(8,128)(2,1)S(1)} %copy-done.2, bf16[32,2,1024]{2,1,0:T(2,128)(2,1)S(1)} %copy-done.3), custom_call_target="tpu_custom_call" | custom-call | tf_op jit(solution)/shard_map/pallas_call | solution.py:71
  5.4 4.3 %all-to-all-start = ((bf16[4,32,4608]{2,1,0:T(8,128)(2,1)}), bf16[4,32,4608]{2,1,0:T(8,128)(2,1)S(1)}, u32[]{:S(2)}, u32[]{:S(2)}) async-start(bf16[4,32,4608]{2,1,0:T(8,128)(2,1)} %shard_map.94), calls=%async_computation | async-start | bytes 2359296 | tf_op jit(solution)/shard_map/all_to_all | solution.py:238
  9.7 0.0 copy-done.4
  9.8 17.3 %all-to-all-done.rows_ref = bf16[4,32,4608]{2,1,0:T(8,128)(2,1)S(1)} async-done(((bf16[4,32,4608]{2,1,0:T(8,128)(2,1)}), bf16[4,32,4608]{2,1,0:T(8,128)(2,1)S(1)}, u32[]{:S(2)}, u32[]{:S(2)}) %all-to-all-start) | async-done | bytes 1179680 | tf_op jit(solution)/shard_map/all_to_all | solution.py:238
  27.1 32.6 %all_to_all.30 = bf16[16,16,512]{2,1,0:T(8,128)(2,1)S(1)} all-to-all(bf16[16,16,512]{2,1,0:T(8,128)(2,1)S(1)} %shard_map.95), channel_id=1, replica_groups=mesh['xl'=2,'z'=16,'y'=4,'xh'=2,'c'=2] {'z'}, dimensions={0} | all-to-all | bytes 524288 | tf_op jit(solution)/shard_map/all_to_all | solution.py:238
  59.7 1.5 broadcast_in_dim.8
  61.2 0.0 copy-start.5
  61.2 0.0 copy-start.6
  61.2 0.0 copy-start.7
  61.2 4.7 %all-to-all-start.2 = ((bf16[8,256,512]{2,1,0:T(8,128)(2,1)}), bf16[8,256,512]{2,1,0:T(8,128)(2,1)S(1)}, u32[]{:S(2)}, u32[]{:S(2)}) async-start(bf16[8,256,512]{2,1,0:T(8,128)(2,1)} %broadcast_in_dim.8), calls=%async_computation.2 | async-start | bytes 4194304 | tf_op jit(solution)/shard_map/all_to_all | solution.py:238
  66.0 22.4 %all-to-all-done.2 = bf16[8,256,512]{2,1,0:T(8,128)(2,1)S(1)} async-done(((bf16[8,256,512]{2,1,0:T(8,128)(2,1)}), bf16[8,256,512]{2,1,0:T(8,128)(2,1)S(1)}, u32[]{:S(2)}, u32[]{:S(2)}) %all-to-all-start.2) | async-done | bytes 2097184 | tf_op jit(solution)/shard_map/all_to_all | solution.py:238
  88.4 0.0 copy-done.5
  88.4 0.0 copy-done.6
  88.4 0.0 copy-done.7
  88.4 4.8 %shard_map.96 = (bf16[4,32,2560]{2,1,0:T(8,128)(2,1)S(1)}, bf16[128,16,512]{2,1,0:T(8,128)(2,1)S(1)}) custom-call(s32[1]{0:T(128)} %bitcast.pos_ref, s32[128]{0:T(128)S(1)} %copy-done.5, s32[128]{0:T(128)S(1)} %copy-done.6, s32[128]{0:T(128)S(1)} %copy-done.7, bf16[4,32,4608]{2,1,0:T(8,128)(2,1)S(1)} %all-to-all-done.rows_ref, bf16[128,16,512]{2,1,0:T(8,128)(2,1)S(1)} %bitcast.5), custom_call_target="tpu_custom_call" | custom-call | flops 1006632960 | bytes 6291456 | tf_op jit(solution)/shard_map/pallas_call | solution.py:216
  93.2 0.0 copy-start
  93.2 30.6 %all_to_all.31.in_ref = bf16[8,256,512]{2,1,0:T(8,128)(2,1)S(1)} all-to-all(bf16[8,256,512]{2,1,0:T(8,128)(2,1)S(1)} %bitcast.6), channel_id=1, replica_groups=mesh['xl'=2,'z'=16,'y'=4,'xh'=2,'c'=2] {'xl','y'}, dimensions={0} | all-to-all | bytes 4194304 | tf_op jit(solution)/shard_map/all_to_all | solution.py:238
  123.8 0.0 copy-done
  123.8 3.5 %all-to-all-start.3 = ((bf16[4,32,2560]{2,1,0:T(8,128)(2,1)}), bf16[4,32,2560]{2,1,0:T(8,128)(2,1)S(1)}, u32[]{:S(2)}, u32[]{:S(2)}) async-start(bf16[4,32,2560]{2,1,0:T(8,128)(2,1)} %copy-done), calls=%async_computation.3 | async-start | bytes 1310720 | tf_op jit(solution)/shard_map/all_to_all | solution.py:238
  127.3 1.0 shard_map.98
  128.2 10.8 %all-to-all-done.3.in_ref = bf16[4,32,2560]{2,1,0:T(8,128)(2,1)S(1)} async-done(((bf16[4,32,2560]{2,1,0:T(8,128)(2,1)}), bf16[4,32,2560]{2,1,0:T(8,128)(2,1)S(1)}, u32[]{:S(2)}, u32[]{:S(2)}) %all-to-all-start.3) | async-done | bytes 655392 | tf_op jit(solution)/shard_map/all_to_all | solution.py:238
  139.0 9.7 %all-to-all-start.5 = ((bf16[16,16,512]{2,1,0:T(8,128)(2,1)}), bf16[16,16,512]{2,1,0:T(8,128)(2,1)S(1)}, u32[]{:S(2)}, u32[]{:S(2)}) async-start(bf16[16,16,512]{2,1,0:T(8,128)(2,1)} %bitcast.4), calls=%async_computation.5 | async-start | bytes 524288 | tf_op jit(solution)/shard_map/all_to_all | solution.py:238
  148.7 1.4 shard_map.97
  150.1 16.6 %all-to-all-done.5.in_ref = bf16[16,16,512]{2,1,0:T(8,128)(2,1)S(1)} async-done(((bf16[16,16,512]{2,1,0:T(8,128)(2,1)}), bf16[16,16,512]{2,1,0:T(8,128)(2,1)S(1)}, u32[]{:S(2)}, u32[]{:S(2)}) %all-to-all-start.5) | async-done | bytes 262176 | tf_op jit(solution)/shard_map/all_to_all | solution.py:238
  166.7 0.7 shard_map.99
  (1 shorter events, 0.0 us)
Async XLA Ops:
  0.6 1.0 copy-start.1
  1.7 1.0 copy-start.2
  2.7 0.9 copy-start.3
  3.6 6.1 %copy-start.4 = (bf16[16,2,256]{2,1,0:T(2,128)(2,1)S(1)}, bf16[16,2,256]{2,1,0:T(2,128)(2,1)}, u32[]{:S(2)}) copy-start(bf16[16,2,256]{2,1,0:T(2,128)(2,1)} %piece_ref.1) | copy-start | bytes 49156
  5.4 21.7 %all-to-all-start = ((bf16[4,32,4608]{2,1,0:T(8,128)(2,1)}), bf16[4,32,4608]{2,1,0:T(8,128)(2,1)S(1)}, u32[]{:S(2)}, u32[]{:S(2)}) async-start(bf16[4,32,4608]{2,1,0:T(8,128)(2,1)} %shard_map.94), calls=%async_computation | async-start | bytes 2359296 | tf_op jit(solution)/shard_map/all_to_all | solution.py:238
  61.2 27.2 %copy-start.5 = (s32[128]{0:T(128)S(1)}, s32[128]{0:T(128)}, u32[]{:S(2)}) copy-start(s32[128]{0:T(128)} %packing_ref.1) | copy-start | bytes 1540
  61.2 27.2 %copy-start.6 = (s32[128]{0:T(128)S(1)}, s32[128]{0:T(128)}, u32[]{:S(2)}) copy-start(s32[128]{0:T(128)} %lengths_ref.1) | copy-start | bytes 1540
  61.2 27.2 %copy-start.7 = (s32[128]{0:T(128)S(1)}, s32[128]{0:T(128)}, u32[]{:S(2)}) copy-start(s32[128]{0:T(128)} %owner_ref.1) | copy-start | bytes 1540
  61.2 27.2 %all-to-all-start.2 = ((bf16[8,256,512]{2,1,0:T(8,128)(2,1)}), bf16[8,256,512]{2,1,0:T(8,128)(2,1)S(1)}, u32[]{:S(2)}, u32[]{:S(2)}) async-start(bf16[8,256,512]{2,1,0:T(8,128)(2,1)} %broadcast_in_dim.8), calls=%async_computation.2 | async-start | bytes 4194304 | tf_op jit(solution)/shard_map/all_to_all | solution.py:238
  93.2 30.6 %copy-start = (bf16[4,32,2560]{2,1,0:T(8,128)(2,1)}, bf16[4,32,2560]{2,1,0:T(8,128)(2,1)S(1)}, u32[]{:S(2)}) copy-start(bf16[4,32,2560]{2,1,0:T(8,128)(2,1)S(1)} %get-tuple-element.7) | copy-start | bytes 1966084
  123.8 15.2 %all-to-all-start.3 = ((bf16[4,32,2560]{2,1,0:T(8,128)(2,1)}), bf16[4,32,2560]{2,1,0:T(8,128)(2,1)S(1)}, u32[]{:S(2)}, u32[]{:S(2)}) async-start(bf16[4,32,2560]{2,1,0:T(8,128)(2,1)} %copy-done), calls=%async_computation.3 | async-start | bytes 1310720 | tf_op jit(solution)/shard_map/all_to_all | solution.py:238
  139.0 27.7 %all-to-all-start.5 = ((bf16[16,16,512]{2,1,0:T(8,128)(2,1)}), bf16[16,16,512]{2,1,0:T(8,128)(2,1)S(1)}, u32[]{:S(2)}, u32[]{:S(2)}) async-start(bf16[16,16,512]{2,1,0:T(8,128)(2,1)} %bitcast.4), calls=%async_computation.5 | async-start | bytes 524288 | tf_op jit(solution)/shard_map/all_to_all | solution.py:238

commit v2 on v1

v2 whole, which is shorter than its diff:
```python
import functools
import math

import jax
import jax.numpy as jnp
from jax import lax
from jax.experimental import pallas as pl
from jax.experimental.pallas import tpu as pltpu
from jax.sharding import Mesh
from jax.sharding import PartitionSpec as P

QUERY_HEADS = 64
KEY_VALUE_HEADS = 8
HEAD = 128
GROUP = 16
PIECE = 16
PROMPT = GROUP * PIECE
SLOTS = 128
KEYS = PROMPT + SLOTS
X_LO, Z, Y = 2, 16, 4
PLANE = X_LO * Y
N_SEQ = PLANE * Z
SLOT_COUNTS = (5, 6, 8, GROUP)
PLANE_IN, PLANE_OUT = (3,), (1,)
N_HEAD = 4
LOCAL_ROWS = SLOTS // N_HEAD
KV_LOCAL = KEY_VALUE_HEADS // N_HEAD
PER_GROUP = QUERY_HEADS // KEY_VALUE_HEADS
Q_WIDTH = KV_LOCAL * PER_GROUP * HEAD
KV_WIDTH = KV_LOCAL * HEAD
IN_WIDTH = 2 * Q_WIDTH + 2 * KV_WIDTH
OUT_WIDTH = Q_WIDTH + 2 * KV_WIDTH
INV_ROOT = 1.0 / math.sqrt(HEAD)
EXP2_SCALE = INV_ROOT / math.log(2.0)

BF16 = jnp.bfloat16
F32 = jnp.float32
PLACE, SOURCE, COUNT, CHOICE = range(4)

SMEM = pl.BlockSpec(memory_space=pltpu.SMEM)
VMEM = pl.BlockSpec(memory_space=pltpu.VMEM)


def params(mib):
    return pltpu.CompilerParams(vmem_limit_bytes=mib * 2**20)


def dot(a, b, contract):
    return lax.dot_general(a, b, (contract, ((), ())), preferred_element_type=F32)


def line_of(s):
    return ((s >> 6) << 2) | (s & 3)


def height_of(s):
    return (s >> 2) & 15


def plan_kernel(place_ref, packing_ref, owner_ref, plan_ref):
    me = place_ref[0]
    square = (N_SEQ, N_SEQ)
    lane = lax.broadcasted_iota(jnp.int32, square, 1)
    row = lax.broadcasted_iota(jnp.int32, square, 0)
    across = jnp.broadcast_to(owner_ref[...], square)
    down = across.T
    same = (line_of(down) == line_of(across)) & ((row >> 4) == (lane >> 4))
    ones = same.astype(jnp.int32)
    most = jnp.max(jnp.sum(ones, axis=0, keepdims=True), axis=1, keepdims=True)
    rank = jnp.sum(jnp.where(row < lane, ones, 0), axis=0, keepdims=True)
    plan_ref[PLACE : PLACE + 1, :] = line_of(owner_ref[...]) * GROUP + rank
    rank_down = jnp.sum(jnp.where(lane < row, ones, 0), axis=1, keepdims=True)
    wanted = jnp.zeros((1, N_SEQ), jnp.int32)
    for d in range(PLANE):
        there = (d // Y) * (Z * Y) + height_of(me) * Y + d % Y
        wanted = jnp.where((lane[:1] >> 4) == d, packing_ref[there] >> 4, wanted)
    held = ((row >> 4) == wanted) & (line_of(down) == line_of(me))
    found = held & (rank_down == (lane & 15))
    plan_ref[SOURCE : SOURCE + 1, :] = jnp.sum(
        jnp.where(found, height_of(down), 0), axis=0, keepdims=True
    )
    plan_ref[COUNT : COUNT + 1, :] = jnp.sum(held.astype(jnp.int32), axis=0, keepdims=True)
    choice = sum((most > n).astype(jnp.int32) for n in SLOT_COUNTS[:-1])
    plan_ref[CHOICE : CHOICE + 1, :] = jnp.broadcast_to(choice, (1, N_SEQ))


def make_plan(place, packing, owner):
    return pl.pallas_call(
        plan_kernel,
        out_shape=jax.ShapeDtypeStruct((4, N_SEQ), jnp.int32),
        in_specs=[SMEM, SMEM, VMEM],
        out_specs=VMEM,
    )(place, packing, owner.reshape(1, N_SEQ))


def select_kernel(slots, plan_ref, line_ref, out_ref):
    for d in range(PLANE):

        @pl.loop(0, plan_ref[COUNT, d * GROUP])
        def _(c, d=d):
            out_ref[d * slots + c] = line_ref[plan_ref[SOURCE, d * GROUP + c]]


def select(plan, line, slots):
    out = pl.pallas_call(
        functools.partial(select_kernel, slots),
        out_shape=jax.ShapeDtypeStruct((PLANE * slots, PIECE, 2 * KV_WIDTH), BF16),
        in_specs=[SMEM, VMEM],
        out_specs=VMEM,
        compiler_params=params(16),
    )(plan, line)
    return out.reshape(PLANE, slots * PIECE, 2 * KV_WIDTH)


def spread_kernel(piece_ref, out_ref):
    flat = jnp.concatenate([piece_ref[:, 0, :], piece_ref[:, 1, :]], axis=1)
    for z in range(Z):
        out_ref[z] = flat


def spread_piece(piece):
    return pl.pallas_call(
        spread_kernel,
        out_shape=jax.ShapeDtypeStruct((Z, PIECE, 2 * KV_WIDTH), BF16),
        in_specs=[VMEM],
        out_specs=VMEM,
        compiler_params=params(16),
    )(piece)


def pack_kernel(place_ref, q_ref, g_ref, kv_ref, *out_refs):
    for k, out_ref in enumerate(out_refs):
        other = place_ref[1] ^ k
        wide = pl.ds(pl.multiple_of(other * Q_WIDTH, Q_WIDTH), Q_WIDTH)
        narrow = pl.ds(pl.multiple_of(other * KV_WIDTH, KV_WIDTH), KV_WIDTH)
        out_ref[:, :Q_WIDTH] = q_ref[:, wide]
        out_ref[:, Q_WIDTH : 2 * Q_WIDTH] = g_ref[:, wide]
        out_ref[:, 2 * Q_WIDTH : 2 * Q_WIDTH + KV_WIDTH] = kv_ref[:, 0, narrow]
        out_ref[:, 2 * Q_WIDTH + KV_WIDTH :] = kv_ref[:, 1, narrow]


def pack_rows(place, queries, grads, kv):
    block = jax.ShapeDtypeStruct((LOCAL_ROWS, IN_WIDTH), BF16)
    return pl.pallas_call(
        pack_kernel,
        out_shape=(block,) * N_HEAD,
        in_specs=[SMEM, VMEM, VMEM, VMEM],
        out_specs=(VMEM,) * N_HEAD,
        compiler_params=params(16),
    )(place, queries, grads, kv)


def unpack_kernel(place_ref, *refs):
    q_ref, kv_ref = refs[N_HEAD:]
    for k, in_ref in enumerate(refs[:N_HEAD]):
        other = place_ref[1] ^ k
        wide = pl.ds(pl.multiple_of(other * Q_WIDTH, Q_WIDTH), Q_WIDTH)
        narrow = pl.ds(pl.multiple_of(other * KV_WIDTH, KV_WIDTH), KV_WIDTH)
        q_ref[:, wide] = in_ref[:, :Q_WIDTH]
        kv_ref[:, 0, narrow] = in_ref[:, Q_WIDTH : Q_WIDTH + KV_WIDTH]
        kv_ref[:, 1, narrow] = in_ref[:, Q_WIDTH + KV_WIDTH :]


def unpack_rows(place, blocks):
    return pl.pallas_call(
        unpack_kernel,
        out_shape=(
            jax.ShapeDtypeStruct((LOCAL_ROWS, N_HEAD * Q_WIDTH), BF16),
            jax.ShapeDtypeStruct((LOCAL_ROWS, 2, N_HEAD * KV_WIDTH), BF16),
        ),
        in_specs=[SMEM] + [VMEM] * N_HEAD,
        out_specs=(VMEM, VMEM),
        compiler_params=params(16),
    )(place, *blocks)


def sum_plane_kernel(slots, plan_ref, part_ref, out_ref, total_ref):
    total_ref[...] = jnp.zeros_like(total_ref)
    for d in range(PLANE):

        @pl.loop(0, plan_ref[COUNT, d * GROUP])
        def _(c, d=d):
            z = plan_ref[SOURCE, d * GROUP + c]
            total_ref[z] = total_ref[z] + part_ref[d * slots + c].astype(F32)

    out_ref[...] = total_ref[...].astype(BF16)


def sum_plane(plan, parts, slots):
    shape = (Z, PIECE, 2 * KV_WIDTH)
    return pl.pallas_call(
        functools.partial(sum_plane_kernel, slots),
        out_shape=jax.ShapeDtypeStruct(shape, BF16),
        in_specs=[SMEM, VMEM],
        out_specs=VMEM,
        scratch_shapes=[pltpu.VMEM(shape, F32)],
        compiler_params=params(16),
    )(plan, parts.reshape(PLANE * slots, PIECE, 2 * KV_WIDTH))


def sum_line_kernel(in_ref, out_ref):
    total = in_ref[0].astype(F32)
    for i in range(1, Z):
        total += in_ref[i].astype(F32)
    out_ref[:, 0, :] = total[:, :KV_WIDTH]
    out_ref[:, 1, :] = total[:, KV_WIDTH:]


def sum_line(parts):
    return pl.pallas_call(
        sum_line_kernel,
        out_shape=jax.ShapeDtypeStruct((PIECE, 2, KV_WIDTH), F32),
        in_specs=[VMEM],
        out_specs=VMEM,
        compiler_params=params(16),
    )(parts)


def slot_index(shape, dim, head):
    row = lax.broadcasted_iota(jnp.int32, shape, dim) % SLOTS
    return ((row // LOCAL_ROWS) ^ head) * LOCAL_ROWS + row % LOCAL_ROWS


def attention_kernel(slots, place_ref, packing_ref, lengths_ref, plan_ref, *refs):
    row_refs, pieces_ref, refs = refs[:N_HEAD], refs[N_HEAD], refs[N_HEAD + 1 :]
    back_refs, grads_ref, refs = refs[:N_HEAD], refs[N_HEAD], refs[N_HEAD + 1 :]
    key_ref, value_ref, weight_ref, dscore_ref = refs

    def rows_of(lo):
        return jnp.concatenate([ref[:, lo : lo + HEAD] for ref in row_refs], axis=0)

    def give_back(block, lo):
        for k, ref in enumerate(back_refs):
            ref[:, lo : lo + HEAD] = block[k * LOCAL_ROWS : (k + 1) * LOCAL_ROWS]

    response = packing_ref[place_ref[0]]
    length = lengths_ref[response]
    first = (response // GROUP) * GROUP
    places = []
    for j in range(GROUP):
        place = plan_ref[PLACE, first + j]
        places.append((place >> 4) * slots + (place & 15))
    for j, at in enumerate(places):
        piece = pieces_ref[at]
        key_ref[j * PIECE : (j + 1) * PIECE, :] = piece[:, :KV_WIDTH]
        value_ref[j * PIECE : (j + 1) * PIECE, :] = piece[:, KV_WIDTH:]
    for g in range(KV_LOCAL):
        cols = slice(g * HEAD, (g + 1) * HEAD)
        key_ref[PROMPT:, cols] = rows_of(2 * Q_WIDTH + g * HEAD)
        value_ref[PROMPT:, cols] = rows_of(2 * Q_WIDTH + KV_WIDTH + g * HEAD)

    pair = 2
    width = pair * SLOTS
    head = place_ref[1]
    query_pos = slot_index((1, width), 1, head)
    causal = slot_index((SLOTS, 1), 0, head) <= query_pos
    used = query_pos < length

    for g in range(KV_LOCAL):
        cols = slice(g * HEAD, (g + 1) * HEAD)
        keys, values = key_ref[:, cols], value_ref[:, cols]
        queries, out_grads = [], []
        for c in range(PER_GROUP // pair):
            at = [(g * PER_GROUP + c * pair + i) * HEAD for i in range(pair)]
            query = jnp.concatenate([rows_of(lo) for lo in at], axis=0)
            out_grad = jnp.concatenate([rows_of(Q_WIDTH + lo) for lo in at], axis=0)
            queries.append(query)
            out_grads.append(out_grad)
            score = dot(keys, query, ((1,), (1,)))
            score = jnp.concatenate(
                [score[:PROMPT], jnp.where(causal, score[PROMPT:], -jnp.inf)], axis=0
            )
            top = jnp.max(score, axis=0, keepdims=True)
            raised = jnp.exp2((score - top) * EXP2_SCALE)
            total = jnp.sum(raised, axis=0, keepdims=True)
            weight = raised * jnp.where(used, 1.0 / total, 0.0)
            weight_half = weight.astype(BF16)
            dprob = dot(values, out_grad, ((1,), (1,)))
            delta = jnp.sum(weight_half.astype(F32) * dprob, axis=0, keepdims=True)
            dscore = (weight * (dprob - delta)).astype(BF16)
            weight_ref[:, c * width : (c + 1) * width] = weight_half
            dscore_ref[:, c * width : (c + 1) * width] = dscore
            query_grad = dot(keys, dscore, ((0,), (0,))).T * INV_ROOT
            for i, lo in enumerate(at):
                give_back(query_grad[i * SLOTS : (i + 1) * SLOTS].astype(BF16), lo)
        key_grad = dot(dscore_ref[...], jnp.concatenate(queries, axis=0), ((1,), (0,))) * INV_ROOT
        value_grad = dot(weight_ref[...], jnp.concatenate(out_grads, axis=0), ((1,), (0,)))
        for slot, grad in enumerate((key_grad, value_grad)):
            grad = grad.astype(BF16)
            lo = slot * KV_WIDTH + g * HEAD
            for j, at in enumerate(places):
                grads_ref[at, :, lo : lo + HEAD] = grad[j * PIECE : (j + 1) * PIECE]
            give_back(grad[PROMPT:], Q_WIDTH + lo)


def attention(place, packing, lengths, plan, rows, pieces, slots):
    flops = 2 * 5 * KEYS * Q_WIDTH // HEAD * SLOTS * HEAD
    block = jax.ShapeDtypeStruct((LOCAL_ROWS, OUT_WIDTH), BF16)
    part = jax.ShapeDtypeStruct((PLANE * slots, PIECE, 2 * KV_WIDTH), BF16)
    out = pl.pallas_call(
        functools.partial(attention_kernel, slots),
        out_shape=(block,) * N_HEAD + (part,),
        in_specs=[SMEM] * 4 + [VMEM] * (N_HEAD + 1),
        out_specs=(VMEM,) * (N_HEAD + 1),
        scratch_shapes=[
            pltpu.VMEM((KEYS, KV_WIDTH), BF16),
            pltpu.VMEM((KEYS, KV_WIDTH), BF16),
            pltpu.VMEM((KEYS, PER_GROUP * SLOTS), BF16),
            pltpu.VMEM((KEYS, PER_GROUP * SLOTS), BF16),
        ],
        compiler_params=params(32),
        cost_estimate=pl.CostEstimate(
            flops=flops, bytes_accessed=6 * 2**20, transcendentals=KEYS * SLOTS * 16
        ),
    )(place, packing, lengths, plan, *rows, pieces.reshape(part.shape))
    return out[:N_HEAD], out[N_HEAD].reshape(PLANE, slots * PIECE, 2 * KV_WIDTH)


def exchange(parts, axes):
    return lax.all_to_all(parts, axes, split_axis=0, concat_axis=0, tiled=True)


def swap(blocks, which):
    return [
        lax.ppermute(block, ("xh", "c"), [(i, i ^ k) for i in range(N_HEAD)])
        if k in which
        else block
        for k, block in enumerate(blocks)
    ]


def shards(queries, out_grads, response_kv, prompt_kv, packing, lengths, owner):
    place = jnp.stack([lax.axis_index(("xl", "z", "y")), lax.axis_index(("xh", "c"))])
    place = place.astype(jnp.int32)
    plane = ("xl", "y")
    others = set(range(1, N_HEAD))
    line = exchange(spread_piece(prompt_kv), "z")
    plan = make_plan(place, packing, owner)
    rows = pack_rows(place, queries, out_grads, response_kv)
    rows = swap(rows, others - set(PLANE_IN))

    def backward(slots, plan, line, *rows):
        pieces = exchange(select(plan, line, slots), plane)
        rows = swap(rows, PLANE_IN)
        back, grads = attention(place, packing, lengths, plan, rows, pieces, slots)
        grads = exchange(grads, plane)
        return swap(back, PLANE_OUT), sum_plane(plan, grads, slots)

    back, grads = lax.switch(
        plan[CHOICE, 0],
        [functools.partial(backward, slots) for slots in SLOT_COUNTS],
        plan, line, *rows,
    )
    grads = exchange(grads, "z")
    back = swap(back, others - set(PLANE_OUT))
    query_grad, resp_grad = unpack_rows(place, back)
    return query_grad, resp_grad, sum_line(grads)


def solution(mesh):
    fine = Mesh(mesh.devices.reshape(X_LO, Z, Y, 2, 2), ("xl", "z", "y", "xh", "c"))
    seq, head = ("xl", "z", "y"), ("xh", "c")
    return jax.shard_map(
        shards,
        mesh=fine,
        in_specs=(
            P(seq + head, None),
            P(seq + head, None),
            P(seq + head, None, None),
            P(seq, None, head),
            P(),
            P(),
            P(),
        ),
        out_specs=(
            P(seq + head, None),
            P(seq + head, None, None),
            P(seq, None, head),
        ),
        check_vma=False,
    )
```

time: 168 us -> 114 us (0.68)
  the two profiles are of different devices: /device:TPU:64 before, /device:TPU:2 now
where the time goes in v2:
time: 114 us; the launch traced here: 113 us
  starting transfers between devices  56.9 us (50%)
  waiting for transfers between devices  36.6 us (32%)
  Pallas kernels  13.6 us (12%)
  local copies, waits for them, and re-layouts  4.22 us (4%)
  between operations  1.37 us (1%)
    all_to_all x4, starting transfers between devices, exchange(): return lax.all_to_all(parts, axes, split_axis=0, concat_axis=0, tiled=True)  38.9 us
    ppermute x6, waiting for transfers between devices, swap(): lax.ppermute(block, ('xh', 'c'), [(i, i ^ k) for i in range(N_HEAD)])  24.6 us
    ppermute x6, starting transfers between devices, swap(): lax.ppermute(block, ('xh', 'c'), [(i, i ^ k) for i in range(N_HEAD)])  18 us
    all_to_all x4, waiting for transfers between devices, exchange(): return lax.all_to_all(parts, axes, split_axis=0, concat_axis=0, tiled=True)  12 us
    pallas_call x1, Pallas kernels, attention(): pl.pallas_call(functools.partial(attention_kernel, slots), out_shape=(blo...  5.51 us
    unnamed x8, local copies, waits for them, and re-layouts  3.7 us
  transfers between devices with their start and end apart: 10, of which 6 were waited for; matrix products, arithmetic and copies ran while one was open for 1% of the time, Pallas kernels for 5%

profile of v2, /device:TPU:2, one launch (start us, length us, event | category | flops | bytes accessed | tf_op | source)
XLA Modules:
  0.0 112.8 jit_solution(6163871254558435878)
XLA Ops:
  0.6 0.0 copy-start.4
  0.6 0.7 copy-done.4
  1.3 0.8 shard_map.96
  2.1 15.2 %all-to-all-start.8 = ((bf16[16,16,512]{2,1,0:T(8,128)(2,1)}), bf16[16,16,512]{2,1,0:T(8,128)(2,1)S(1)}, u32[]{:S(2)}, u32[]{:S(2)}) async-start(bf16[16,16,512]{2,1,0:T(8,128)(2,1)} %shard_map.96), calls=%async_computation.8 | async-start | bytes 524288 | tf_op jit(solution)/shard_map/all_to_all | solution.py:320
  17.3 0.1 pad_add_fusion.place_ref
  17.4 0.0 copy-start.1
  17.4 1.0 copy-done.1
  18.4 0.0 copy-start.2
  18.4 1.0 copy-done.2
  19.5 0.0 copy-start.3
  19.5 0.9 copy-done.3
  20.4 0.8 shard_map.95
  21.2 1.9 %collective-permute-start.8 = (bf16[32,4608]{1,0:T(8,128)(2,1)S(1)}, bf16[32,4608]{1,0:T(8,128)(2,1)S(1)}, u32[]{:S(2)}, u32[]{:S(2)}) collective-permute-start(bf16[32,4608]{1,0:T(8,128)(2,1)S(1)} %get-tuple-element.144), channel_id=1, source_target_pairs={{0,1},{1,0},{2,3},{3,2},{4,5},{5,4},{6,7},{7,6},{8,9},{9,8},{10,11... | collective-permute-start | bytes 884744 | tf_op jit(solution)/shard_map/ppermute | solution.py:325
  23.1 4.0 %collective-permute-start.9 = (bf16[32,4608]{1,0:T(8,128)(2,1)S(1)}, bf16[32,4608]{1,0:T(8,128)(2,1)S(1)}, u32[]{:S(2)}, u32[]{:S(2)}) collective-permute-start(bf16[32,4608]{1,0:T(8,128)(2,1)S(1)} %get-tuple-element.145), channel_id=1, source_target_pairs={{0,2},{1,3},{2,0},{3,1},{4,6},{5,7},{6,4},{7,5},{8,10},{9,11},{10,... | collective-permute-start | bytes 884744 | tf_op jit(solution)/shard_map/ppermute | solution.py:325
  27.2 0.9 shard_map.94
  28.1 0.5 slice.3
  29.3 0.0 collective-permute-done.8
  29.3 6.6 %collective-permute-done.9 = bf16[32,4608]{1,0:T(8,128)(2,1)S(1)} collective-permute-done((bf16[32,4608]{1,0:T(8,128)(2,1)S(1)}, bf16[32,4608]{1,0:T(8,128)(2,1)S(1)}, u32[]{:S(2)}, u32[]{:S(2)}) %collective-permute-start.9) | collective-permute-done | bytes 294944 | tf_op jit(solution)/shard_map/ppermute | solution.py:325
  36.0 0.0 all-to-all-done.8
  36.0 45.6 %conditional.1 = (bf16[32,2560]{1,0:T(8,128)(2,1)S(1)}, bf16[32,2560]{1,0:T(8,128)(2,1)}, bf16[32,2560]{1,0:T(8,128)(2,1)}, bf16[32,2560]{1,0:T(8,128)(2,1)}, bf16[16,16,512]{2,1,0:T(8,128)(2,1)}) conditional(s32[]{:T(128)} %bitcast.19, (bf16[32,4608]{1,0:T(8,128)(2,1)S(1)}, s32[4,128]{1,0:T(4,128)S(1)}, ...), branch_computations={%region_0.0_spmd, %region_1.0_spmd, %region_2.0_spmd, %region_3.0_... | conditional | flops 1006632960 | bytes 30282024 | solution.py:349
  36.0 0.0 copy-start.5
  36.0 0.0 copy-start.10
  36.0 1.6 %branch_0_fun.3 = bf16[40,16,512]{2,1,0:T(8,128)(2,1)} custom-call(s32[4,128]{1,0:T(4,128)S(1)} %get-tuple-element.75.plan_ref, bf16[16,16,512]{2,1,0:T(8,128)(2,1)S(1)} %get-tuple-element.80.line_ref), custom_call_target="tpu_custom_call" | custom-call | tf_op jit(solution)/shard_map/cond/branch_0_fun/pallas_call | solution.py:105
  37.5 6.0 %all-to-all-start = ((bf16[8,80,512]{2,1,0:T(8,128)(2,1)}), bf16[8,80,512]{2,1,0:T(8,128)(2,1)S(1)}, u32[]{:S(2)}, u32[]{:S(2)}) async-start(bf16[8,80,512]{2,1,0:T(8,128)(2,1)} %bitcast), calls=%async_computation | async-start | bytes 1310720 | tf_op jit(solution)/shard_map/cond/branch_0_fun/all_to_all | solution.py:320
  43.5 2.8 %collective-permute-start = (bf16[32,4608]{1,0:T(8,128)(2,1)S(1)}, bf16[32,4608]{1,0:T(8,128)(2,1)S(1)}, u32[]{:S(2)}, u32[]{:S(2)}) collective-permute-start(bf16[32,4608]{1,0:T(8,128)(2,1)S(1)} %get-tuple-element.79), channel_id=1, source_target_pairs={{0,3},{1,2},{2,1},{3,0},{4,7},{5,6},{6,5},{7,4},{8,11},{9,10},{10,... | collective-permute-start | bytes 884744 | tf_op jit(solution)/shard_map/cond/branch_0_fun/ppermute | solution.py:325
  46.3 11.3 %collective-permute-done.refs_3_ = bf16[32,4608]{1,0:T(8,128)(2,1)S(1)} collective-permute-done((bf16[32,4608]{1,0:T(8,128)(2,1)S(1)}, bf16[32,4608]{1,0:T(8,128)(2,1)S(1)}, u32[]{:S(2)}, u32[]{:S(2)}) %collective-permute-start) | collective-permute-done | bytes 294944 | tf_op jit(solution)/shard_map/cond/branch_0_fun/ppermute | solution.py:325
  57.6 0.0 all-to-all-done
  57.6 0.0 copy-done.5
  57.6 0.0 copy-done.10
  57.6 5.5 %branch_0_fun.4 = (bf16[32,2560]{1,0:T(8,128)(2,1)S(1)}, bf16[32,2560]{1,0:T(8,128)(2,1)S(1)}, bf16[32,2560]{1,0:T(8,128)(2,1)}, bf16[32,2560]{1,0:T(8,128)(2,1)}, bf16[40,16,512]{2,1,0:T(8,128)(2,1)}) custom-call(s32[2]{0:T(128)S(1)} %get-tuple-element.72.place_ref, s32[128]{0:T(128)S(1)} %copy-done.5, s32[128]{0:T(128)S(1)} %copy-done.10, ...), custom_call_target="tpu_custom_call" | custom-call | flops 1006632960 | bytes 6291456 | tf_op jit(solution)/shard_map/cond/branch_0_fun/pallas_call | solution.py:300
  63.1 5.7 %all-to-all-start.1 = ((bf16[8,80,512]{2,1,0:T(8,128)(2,1)}), bf16[8,80,512]{2,1,0:T(8,128)(2,1)S(1)}, u32[]{:S(2)}, u32[]{:S(2)}) async-start(bf16[8,80,512]{2,1,0:T(8,128)(2,1)} %bitcast.2), calls=%async_computation.1 | async-start | bytes 1310720 | tf_op jit(solution)/shard_map/cond/branch_0_fun/all_to_all | solution.py:320
  68.8 2.8 %collective-permute-start.1 = (bf16[32,2560]{1,0:T(8,128)(2,1)S(1)}, bf16[32,2560]{1,0:T(8,128)(2,1)}, u32[]{:S(2)}, u32[]{:S(2)}) collective-permute-start(bf16[32,2560]{1,0:T(8,128)(2,1)S(1)} %get-tuple-element.82), channel_id=1, source_target_pairs={{0,1},{1,0},{2,3},{3,2},{4,5},{5,4},{6,7},{7,6},{8,9},{9,8},{10,11... | collective-permute-start | bytes 491528 | tf_op jit(solution)/shard_map/cond/branch_0_fun/ppermute | solution.py:325
  71.6 8.5 %all-to-all-done.1 = bf16[8,80,512]{2,1,0:T(8,128)(2,1)S(1)} async-done(((bf16[8,80,512]{2,1,0:T(8,128)(2,1)}), bf16[8,80,512]{2,1,0:T(8,128)(2,1)S(1)}, u32[]{:S(2)}, u32[]{:S(2)}) %all-to-all-start.1) | async-done | bytes 655392 | tf_op jit(solution)/shard_map/cond/branch_0_fun/all_to_all | solution.py:320
  80.1 1.5 %branch_0_fun.5 = bf16[16,16,512]{2,1,0:T(8,128)(2,1)} custom-call(s32[4,128]{1,0:T(4,128)S(1)} %get-tuple-element.75.plan_ref, bf16[40,16,512]{2,1,0:T(8,128)(2,1)S(1)} %bitcast.23), custom_call_target="tpu_custom_call" | custom-call | tf_op jit(solution)/shard_map/cond/branch_0_fun/pallas_call | solution.py:191
  81.6 0.0 collective-permute-done.1
  81.6 12.0 %all-to-all-start.9 = ((bf16[16,16,512]{2,1,0:T(8,128)(2,1)}), bf16[16,16,512]{2,1,0:T(8,128)(2,1)S(1)}, u32[]{:S(2)}, u32[]{:S(2)}) async-start(bf16[16,16,512]{2,1,0:T(8,128)(2,1)} %get-tuple-element.152), calls=%async_computation.9 | async-start | bytes 524288 | tf_op jit(solution)/shard_map/all_to_all | solution.py:320
  93.7 3.3 %collective-permute-start.10 = (bf16[32,2560]{1,0:T(8,128)(2,1)}, bf16[32,2560]{1,0:T(8,128)(2,1)S(1)}, u32[]{:S(2)}, u32[]{:S(2)}) collective-permute-start(bf16[32,2560]{1,0:T(8,128)(2,1)} %get-tuple-element.148), channel_id=1, source_target_pairs={{0,2},{1,3},{2,0},{3,1},{4,6},{5,7},{6,4},{7,5},{8,10},{9,11},{10,... | collective-permute-start | bytes 491528 | tf_op jit(solution)/shard_map/ppermute | solution.py:325
  97.0 3.2 %collective-permute-start.11 = (bf16[32,2560]{1,0:T(8,128)(2,1)}, bf16[32,2560]{1,0:T(8,128)(2,1)S(1)}, u32[]{:S(2)}, u32[]{:S(2)}) collective-permute-start(bf16[32,2560]{1,0:T(8,128)(2,1)} %get-tuple-element.149), channel_id=1, source_target_pairs={{0,3},{1,2},{2,1},{3,0},{4,7},{5,6},{6,5},{7,4},{8,11},{9,10},{10,... | collective-permute-start | bytes 491528 | tf_op jit(solution)/shard_map/ppermute | solution.py:325
  100.2 3.0 %collective-permute-done.10.refs_2_ = bf16[32,2560]{1,0:T(8,128)(2,1)S(1)} collective-permute-done((bf16[32,2560]{1,0:T(8,128)(2,1)}, bf16[32,2560]{1,0:T(8,128)(2,1)S(1)}, u32[]{:S(2)}, u32[]{:S(2)}) %collective-permute-start.10) | collective-permute-done | bytes 163872 | tf_op jit(solution)/shard_map/ppermute | solution.py:325
  103.2 3.6 %collective-permute-done.11.refs_3_ = bf16[32,2560]{1,0:T(8,128)(2,1)S(1)} collective-permute-done((bf16[32,2560]{1,0:T(8,128)(2,1)}, bf16[32,2560]{1,0:T(8,128)(2,1)S(1)}, u32[]{:S(2)}, u32[]{:S(2)}) %collective-permute-start.11) | collective-permute-done | bytes 163872 | tf_op jit(solution)/shard_map/ppermute | solution.py:325
  106.8 1.8 %shard_map.97 = (bf16[32,8192]{1,0:T(8,128)(2,1)}, bf16[32,2,1024]{2,1,0:T(2,128)(2,1)}) custom-call(s32[2]{0:T(128)S(1)} %pad_add_fusion.place_ref, bf16[32,2560]{1,0:T(8,128)(2,1)S(1)} %get-tuple-element.146.refs_0_, bf16[32,2560]{1,0:T(8,128)(2,1)} %get-tuple-element.147.refs_1_, bf16[32,2560]{1,0:T(8,128)(2,1)S(1)} %collective-permute-done.10.refs_2_, ...), custom_call_target="tpu_custom_call" | custom-call | tf_op jit(solution)/shard_map/pallas_call | solution.py:165
  108.6 3.5 %all-to-all-done.9.in_ref = bf16[16,16,512]{2,1,0:T(8,128)(2,1)S(1)} async-done(((bf16[16,16,512]{2,1,0:T(8,128)(2,1)}), bf16[16,16,512]{2,1,0:T(8,128)(2,1)S(1)}, u32[]{:S(2)}, u32[]{:S(2)}) %all-to-all-start.9) | async-done | bytes 262176 | tf_op jit(solution)/shard_map/all_to_all | solution.py:320
  112.1 0.7 shard_map.98
Async XLA Ops:
  0.6 0.7 copy-start.4
  2.1 33.9 %all-to-all-start.8 = ((bf16[16,16,512]{2,1,0:T(8,128)(2,1)}), bf16[16,16,512]{2,1,0:T(8,128)(2,1)S(1)}, u32[]{:S(2)}, u32[]{:S(2)}) async-start(bf16[16,16,512]{2,1,0:T(8,128)(2,1)} %shard_map.96), calls=%async_computation.8 | async-start | bytes 524288 | tf_op jit(solution)/shard_map/all_to_all | solution.py:320
  17.4 1.0 copy-start.1
  18.4 1.0 copy-start.2
  19.5 0.9 copy-start.3
  21.2 8.1 %collective-permute-start.8 = (bf16[32,4608]{1,0:T(8,128)(2,1)S(1)}, bf16[32,4608]{1,0:T(8,128)(2,1)S(1)}, u32[]{:S(2)}, u32[]{:S(2)}) collective-permute-start(bf16[32,4608]{1,0:T(8,128)(2,1)S(1)} %get-tuple-element.144), channel_id=1, source_target_pairs={{0,1},{1,0},{2,3},{3,2},{4,5},{5,4},{6,7},{7,6},{8,9},{9,8},{10,11... | collective-permute-start | bytes 884744 | tf_op jit(solution)/shard_map/ppermute | solution.py:325
  23.1 12.8 %collective-permute-start.9 = (bf16[32,4608]{1,0:T(8,128)(2,1)S(1)}, bf16[32,4608]{1,0:T(8,128)(2,1)S(1)}, u32[]{:S(2)}, u32[]{:S(2)}) collective-permute-start(bf16[32,4608]{1,0:T(8,128)(2,1)S(1)} %get-tuple-element.145), channel_id=1, source_target_pairs={{0,2},{1,3},{2,0},{3,1},{4,6},{5,7},{6,4},{7,5},{8,10},{9,11},{10,... | collective-permute-start | bytes 884744 | tf_op jit(solution)/shard_map/ppermute | solution.py:325
  36.0 21.6 %copy-start.5 = (s32[128]{0:T(128)S(1)}, s32[128]{0:T(128)}, u32[]{:S(2)}) copy-start(s32[128]{0:T(128)} %get-tuple-element.73.packing_ref) | copy-start | bytes 1540 | tf_op jit(solution)/shard_map/cond
  36.0 21.6 %copy-start.10 = (s32[128]{0:T(128)S(1)}, s32[128]{0:T(128)}, u32[]{:S(2)}) copy-start(s32[128]{0:T(128)} %get-tuple-element.74.lengths_ref) | copy-start | bytes 1540 | tf_op jit(solution)/shard_map/cond
  37.5 20.0 %all-to-all-start = ((bf16[8,80,512]{2,1,0:T(8,128)(2,1)}), bf16[8,80,512]{2,1,0:T(8,128)(2,1)S(1)}, u32[]{:S(2)}, u32[]{:S(2)}) async-start(bf16[8,80,512]{2,1,0:T(8,128)(2,1)} %bitcast), calls=%async_computation | async-start | bytes 1310720 | tf_op jit(solution)/shard_map/cond/branch_0_fun/all_to_all | solution.py:320
  43.5 14.1 %collective-permute-start = (bf16[32,4608]{1,0:T(8,128)(2,1)S(1)}, bf16[32,4608]{1,0:T(8,128)(2,1)S(1)}, u32[]{:S(2)}, u32[]{:S(2)}) collective-permute-start(bf16[32,4608]{1,0:T(8,128)(2,1)S(1)} %get-tuple-element.79), channel_id=1, source_target_pairs={{0,3},{1,2},{2,1},{3,0},{4,7},{5,6},{6,5},{7,4},{8,11},{9,10},{10,... | collective-permute-start | bytes 884744 | tf_op jit(solution)/shard_map/cond/branch_0_fun/ppermute | solution.py:325
  63.1 17.0 %all-to-all-start.1 = ((bf16[8,80,512]{2,1,0:T(8,128)(2,1)}), bf16[8,80,512]{2,1,0:T(8,128)(2,1)S(1)}, u32[]{:S(2)}, u32[]{:S(2)}) async-start(bf16[8,80,512]{2,1,0:T(8,128)(2,1)} %bitcast.2), calls=%async_computation.1 | async-start | bytes 1310720 | tf_op jit(solution)/shard_map/cond/branch_0_fun/all_to_all | solution.py:320
  68.8 12.8 %collective-permute-start.1 = (bf16[32,2560]{1,0:T(8,128)(2,1)S(1)}, bf16[32,2560]{1,0:T(8,128)(2,1)}, u32[]{:S(2)}, u32[]{:S(2)}) collective-permute-start(bf16[32,2560]{1,0:T(8,128)(2,1)S(1)} %get-tuple-element.82), channel_id=1, source_target_pairs={{0,1},{1,0},{2,3},{3,2},{4,5},{5,4},{6,7},{7,6},{8,9},{9,8},{10,11... | collective-permute-start | bytes 491528 | tf_op jit(solution)/shard_map/cond/branch_0_fun/ppermute | solution.py:325
  81.6 30.5 %all-to-all-start.9 = ((bf16[16,16,512]{2,1,0:T(8,128)(2,1)}), bf16[16,16,512]{2,1,0:T(8,128)(2,1)S(1)}, u32[]{:S(2)}, u32[]{:S(2)}) async-start(bf16[16,16,512]{2,1,0:T(8,128)(2,1)} %get-tuple-element.152), calls=%async_computation.9 | async-start | bytes 524288 | tf_op jit(solution)/shard_map/all_to_all | solution.py:320
  93.7 9.5 %collective-permute-start.10 = (bf16[32,2560]{1,0:T(8,128)(2,1)}, bf16[32,2560]{1,0:T(8,128)(2,1)S(1)}, u32[]{:S(2)}, u32[]{:S(2)}) collective-permute-start(bf16[32,2560]{1,0:T(8,128)(2,1)} %get-tuple-element.148), channel_id=1, source_target_pairs={{0,2},{1,3},{2,0},{3,1},{4,6},{5,7},{6,4},{7,5},{8,10},{9,11},{10,... | collective-permute-start | bytes 491528 | tf_op jit(solution)/shard_map/ppermute | solution.py:325
  97.0 9.8 %collective-permute-start.11 = (bf16[32,2560]{1,0:T(8,128)(2,1)}, bf16[32,2560]{1,0:T(8,128)(2,1)S(1)}, u32[]{:S(2)}, u32[]{:S(2)}) collective-permute-start(bf16[32,2560]{1,0:T(8,128)(2,1)} %get-tuple-element.149), channel_id=1, source_target_pairs={{0,3},{1,2},{2,1},{3,0},{4,7},{5,6},{6,5},{7,4},{8,11},{9,10},{10,... | collective-permute-start | bytes 491528 | tf_op jit(solution)/shard_map/ppermute | solution.py:325

commit v3 on v2

--- a/solution.py
+++ b/solution.py
@@ -20,8 +20,7 @@
 X_LO, Z, Y = 2, 16, 4
 PLANE = X_LO * Y
 N_SEQ = PLANE * Z
-SLOT_COUNTS = (5, 6, 8, GROUP)
-PLANE_IN, PLANE_OUT = (3,), (1,)
+SLOT_COUNTS = (4, 5, 6, 7, 8, GROUP)
 N_HEAD = 4
 LOCAL_ROWS = SLOTS // N_HEAD
 KV_LOCAL = KEY_VALUE_HEADS // N_HEAD
@@ -30,6 +29,7 @@
 KV_WIDTH = KV_LOCAL * HEAD
 IN_WIDTH = 2 * Q_WIDTH + 2 * KV_WIDTH
 OUT_WIDTH = Q_WIDTH + 2 * KV_WIDTH
+CHUNK, STRIP = 8, 64
 INV_ROOT = 1.0 / math.sqrt(HEAD)
 EXP2_SCALE = INV_ROOT / math.log(2.0)
 
@@ -112,47 +112,53 @@
     return out.reshape(PLANE, slots * PIECE, 2 * KV_WIDTH)
 
 
-def spread_kernel(piece_ref, out_ref):
-    flat = jnp.concatenate([piece_ref[:, 0, :], piece_ref[:, 1, :]], axis=1)
+def pack_kernel(place_ref, q_ref, g_ref, kv_ref, piece_ref, *refs):
+    row_refs, line_ref, kv_here, piece_here, sems = refs[:N_HEAD], *refs[N_HEAD:]
+    fetch_piece = pltpu.make_async_copy(piece_ref, piece_here, sems.at[0])
+    fetch_kv = pltpu.make_async_copy(kv_ref, kv_here, sems.at[1])
+    fetch_piece.start()
+    fetch_kv.start()
+    others = [place_ref[1] ^ k for k in range(N_HEAD)]
+    fetches = []
+    for k, (other, out_ref) in enumerate(zip(others, row_refs)):
+        wide = pl.ds(pl.multiple_of(other * Q_WIDTH, Q_WIDTH), Q_WIDTH)
+        for i, ref in enumerate((q_ref, g_ref)):
+            here = out_ref.at[:, i * Q_WIDTH : (i + 1) * Q_WIDTH]
+            fetches.append(pltpu.make_async_copy(ref.at[:, wide], here, sems.at[2 + 2 * k + i]))
+            fetches[-1].start()
+    fetch_piece.wait()
+    flat = jnp.concatenate([piece_here[:, 0, :], piece_here[:, 1, :]], axis=1)
     for z in range(Z):
-        out_ref[z] = flat
-
-
-def spread_piece(piece):
-    return pl.pallas_call(
-        spread_kernel,
-        out_shape=jax.ShapeDtypeStruct((Z, PIECE, 2 * KV_WIDTH), BF16),
-        in_specs=[VMEM],
-        out_specs=VMEM,
-        compiler_params=params(16),
-    )(piece)
-
-
-def pack_kernel(place_ref, q_ref, g_ref, kv_ref, *out_refs):
-    for k, out_ref in enumerate(out_refs):
-        other = place_ref[1] ^ k
-        wide = pl.ds(pl.multiple_of(other * Q_WIDTH, Q_WIDTH), Q_WIDTH)
+        line_ref[z] = flat
+    fetch_kv.wait()
+    for other, out_ref in zip(others, row_refs):
         narrow = pl.ds(pl.multiple_of(other * KV_WIDTH, KV_WIDTH), KV_WIDTH)
-        out_ref[:, :Q_WIDTH] = q_ref[:, wide]
-        out_ref[:, Q_WIDTH : 2 * Q_WIDTH] = g_ref[:, wide]
-        out_ref[:, 2 * Q_WIDTH : 2 * Q_WIDTH + KV_WIDTH] = kv_ref[:, 0, narrow]
-        out_ref[:, 2 * Q_WIDTH + KV_WIDTH :] = kv_ref[:, 1, narrow]
-
-
-def pack_rows(place, queries, grads, kv):
-    block = jax.ShapeDtypeStruct((LOCAL_ROWS, IN_WIDTH), BF16)
+        for i in range(2):
+            lo = 2 * Q_WIDTH + i * KV_WIDTH
+            out_ref[:, lo : lo + KV_WIDTH] = kv_here[:, i, narrow]
+    for fetch in fetches:
+        fetch.wait()
+
+
+def pack(place, queries, grads, kv, piece):
     return pl.pallas_call(
         pack_kernel,
-        out_shape=(block,) * N_HEAD,
-        in_specs=[SMEM, VMEM, VMEM, VMEM],
-        out_specs=(VMEM,) * N_HEAD,
-        compiler_params=params(16),
-    )(place, queries, grads, kv)
+        out_shape=(jax.ShapeDtypeStruct((LOCAL_ROWS, IN_WIDTH), BF16),) * N_HEAD
+        + (jax.ShapeDtypeStruct((Z, PIECE, 2 * KV_WIDTH), BF16),),
+        in_specs=[SMEM] + [pl.BlockSpec(memory_space=pltpu.HBM)] * 4,
+        out_specs=(VMEM,) * (N_HEAD + 1),
+        scratch_shapes=[
+            pltpu.VMEM(kv.shape, BF16),
+            pltpu.VMEM(piece.shape, BF16),
+            pltpu.SemaphoreType.DMA((2 + 2 * N_HEAD,)),
+        ],
+        compiler_params=params(16),
+    )(place, *[pltpu.with_memory_space_constraint(x, pltpu.HBM) for x in (queries, grads, kv, piece)])
 
 
 def unpack_kernel(place_ref, *refs):
     q_ref, kv_ref = refs[N_HEAD:]
-    for k, in_ref in enumerate(refs[:N_HEAD]):
+    for k, in_ref in enumerate(refs[N_HEAD - 1 :: -1]):
         other = place_ref[1] ^ k
         wide = pl.ds(pl.multiple_of(other * Q_WIDTH, Q_WIDTH), Q_WIDTH)
         narrow = pl.ds(pl.multiple_of(other * KV_WIDTH, KV_WIDTH), KV_WIDTH)
@@ -171,7 +177,44 @@
         in_specs=[SMEM] + [VMEM] * N_HEAD,
         out_specs=(VMEM, VMEM),
         compiler_params=params(16),
-    )(place, *blocks)
+    )(place, *reversed(blocks))
+
+
+def slots_of(place_ref, packing_ref, plan_ref, slots):
+    first = (packing_ref[place_ref[0]] >> 4) << 4
+    places = [plan_ref[PLACE, first + j] for j in range(GROUP)]
+    return [(place >> 4) * slots + (place & 15) for place in places]
+
+
+def collect_kernel(slots, place_ref, packing_ref, plan_ref, parts_ref, out_ref):
+    for j, at in enumerate(slots_of(place_ref, packing_ref, plan_ref, slots)):
+        out_ref[j * PIECE : (j + 1) * PIECE] = parts_ref[at]
+
+
+def collect(place, packing, plan, parts, slots):
+    return pl.pallas_call(
+        functools.partial(collect_kernel, slots),
+        out_shape=jax.ShapeDtypeStruct((PROMPT, 2 * KV_WIDTH), BF16),
+        in_specs=[SMEM, SMEM, SMEM, VMEM],
+        out_specs=VMEM,
+        compiler_params=params(16),
+    )(place, packing, plan, parts.reshape(PLANE * slots, PIECE, 2 * KV_WIDTH))
+
+
+def scatter_kernel(slots, place_ref, packing_ref, plan_ref, rows_ref, out_ref):
+    for j, at in enumerate(slots_of(place_ref, packing_ref, plan_ref, slots)):
+        out_ref[at] = rows_ref[j * PIECE : (j + 1) * PIECE]
+
+
+def scatter(place, packing, plan, rows, slots):
+    out = pl.pallas_call(
+        functools.partial(scatter_kernel, slots),
+        out_shape=jax.ShapeDtypeStruct((PLANE * slots, PIECE, 2 * KV_WIDTH), BF16),
+        in_specs=[SMEM, SMEM, SMEM, VMEM],
+        out_specs=VMEM,
+        compiler_params=params(16),
+    )(place, packing, plan, rows)
+    return out.reshape(PLANE, slots * PIECE, 2 * KV_WIDTH)
 
 
 def sum_plane_kernel(slots, plan_ref, part_ref, out_ref, total_ref):
@@ -216,13 +259,13 @@
     )(parts)
 
 
-def slot_index(shape, dim, head):
-    row = lax.broadcasted_iota(jnp.int32, shape, dim) % SLOTS
+def slot_index(shape, dim, head, first=0):
+    row = (lax.broadcasted_iota(jnp.int32, shape, dim) + first) % SLOTS
     return ((row // LOCAL_ROWS) ^ head) * LOCAL_ROWS + row % LOCAL_ROWS
 
 
-def attention_kernel(slots, place_ref, packing_ref, lengths_ref, plan_ref, *refs):
-    row_refs, pieces_ref, refs = refs[:N_HEAD], refs[N_HEAD], refs[N_HEAD + 1 :]
+def attention_kernel(place_ref, packing_ref, lengths_ref, *refs):
+    row_refs, prompt_ref, refs = refs[N_HEAD - 1 :: -1], refs[N_HEAD], refs[N_HEAD + 1 :]
     back_refs, grads_ref, refs = refs[:N_HEAD], refs[N_HEAD], refs[N_HEAD + 1 :]
     key_ref, value_ref, weight_ref, dscore_ref = refs
 
@@ -233,74 +276,82 @@
         for k, ref in enumerate(back_refs):
             ref[:, lo : lo + HEAD] = block[k * LOCAL_ROWS : (k + 1) * LOCAL_ROWS]
 
-    response = packing_ref[place_ref[0]]
-    length = lengths_ref[response]
-    first = (response // GROUP) * GROUP
-    places = []
-    for j in range(GROUP):
-        place = plan_ref[PLACE, first + j]
-        places.append((place >> 4) * slots + (place & 15))
-    for j, at in enumerate(places):
-        piece = pieces_ref[at]
-        key_ref[j * PIECE : (j + 1) * PIECE, :] = piece[:, :KV_WIDTH]
-        value_ref[j * PIECE : (j + 1) * PIECE, :] = piece[:, KV_WIDTH:]
+    length = lengths_ref[packing_ref[place_ref[0]]]
+    key_ref[:PROMPT] = prompt_ref[:, :KV_WIDTH]
+    value_ref[:PROMPT] = prompt_ref[:, KV_WIDTH:]
     for g in range(KV_LOCAL):
         cols = slice(g * HEAD, (g + 1) * HEAD)
         key_ref[PROMPT:, cols] = rows_of(2 * Q_WIDTH + g * HEAD)
         value_ref[PROMPT:, cols] = rows_of(2 * Q_WIDTH + KV_WIDTH + g * HEAD)
 
-    pair = 2
-    width = pair * SLOTS
+    width = CHUNK * SLOTS
     head = place_ref[1]
     query_pos = slot_index((1, width), 1, head)
-    causal = slot_index((SLOTS, 1), 0, head) <= query_pos
     used = query_pos < length
+    strips = [slice(lo, lo + STRIP) for lo in range(0, KEYS, STRIP)]
+
+    def fold(x):
+        return jnp.sum(x.reshape(STRIP // 8, 8, width), axis=0)
 
     for g in range(KV_LOCAL):
         cols = slice(g * HEAD, (g + 1) * HEAD)
         keys, values = key_ref[:, cols], value_ref[:, cols]
+        keys_down = keys.T
         queries, out_grads = [], []
-        for c in range(PER_GROUP // pair):
-            at = [(g * PER_GROUP + c * pair + i) * HEAD for i in range(pair)]
+        for c in range(PER_GROUP // CHUNK):
+            at = [(g * PER_GROUP + c * CHUNK + i) * HEAD for i in range(CHUNK)]
             query = jnp.concatenate([rows_of(lo) for lo in at], axis=0)
             out_grad = jnp.concatenate([rows_of(Q_WIDTH + lo) for lo in at], axis=0)
             queries.append(query)
             out_grads.append(out_grad)
             score = dot(keys, query, ((1,), (1,)))
-            score = jnp.concatenate(
-                [score[:PROMPT], jnp.where(causal, score[PROMPT:], -jnp.inf)], axis=0
-            )
-            top = jnp.max(score, axis=0, keepdims=True)
-            raised = jnp.exp2((score - top) * EXP2_SCALE)
-            total = jnp.sum(raised, axis=0, keepdims=True)
-            weight = raised * jnp.where(used, 1.0 / total, 0.0)
-            weight_half = weight.astype(BF16)
             dprob = dot(values, out_grad, ((1,), (1,)))
-            delta = jnp.sum(weight_half.astype(F32) * dprob, axis=0, keepdims=True)
-            dscore = (weight * (dprob - delta)).astype(BF16)
-            weight_ref[:, c * width : (c + 1) * width] = weight_half
-            dscore_ref[:, c * width : (c + 1) * width] = dscore
-            query_grad = dot(keys, dscore, ((0,), (0,))).T * INV_ROOT
+            top = None
+            scores = []
+            for strip in strips:
+                part = score[strip]
+                if strip.start >= PROMPT:
+                    key_pos = slot_index((STRIP, 1), 0, head, strip.start - PROMPT)
+                    part = jnp.where(key_pos <= query_pos, part, -jnp.inf)
+                scores.append(part)
+                most = jnp.max(part.reshape(STRIP // 8, 8, width), axis=0)
+                top = most if top is None else jnp.maximum(top, most)
+            shift = jnp.max(top, axis=0, keepdims=True) * EXP2_SCALE
+            raised, total, moment = [], 0.0, 0.0
+            for strip, part in zip(strips, scores):
+                part = jnp.exp2(part * EXP2_SCALE - shift)
+                raised.append(part)
+                total += fold(part)
+                moment += fold(part * dprob[strip])
+            total = jnp.sum(total, axis=0, keepdims=True)
+            moment = jnp.sum(moment, axis=0, keepdims=True)
+            scale = jnp.where(used, 1.0 / total, 0.0)
+            delta = moment * scale
+            here = slice(c * width, (c + 1) * width)
+            for strip, part in zip(strips, raised):
+                weight = part * scale
+                weight_ref[strip, here] = weight.astype(BF16)
+                dscore_ref[strip, here] = (weight * (dprob[strip] - delta)).astype(BF16)
+            query_grad = dot(keys_down, dscore_ref[:, here], ((1,), (0,)))
+            query_grad = (query_grad * INV_ROOT).astype(BF16).T
             for i, lo in enumerate(at):
-                give_back(query_grad[i * SLOTS : (i + 1) * SLOTS].astype(BF16), lo)
+                give_back(query_grad[i * SLOTS : (i + 1) * SLOTS], lo)
         key_grad = dot(dscore_ref[...], jnp.concatenate(queries, axis=0), ((1,), (0,))) * INV_ROOT
         value_grad = dot(weight_ref[...], jnp.concatenate(out_grads, axis=0), ((1,), (0,)))
         for slot, grad in enumerate((key_grad, value_grad)):
             grad = grad.astype(BF16)
             lo = slot * KV_WIDTH + g * HEAD
-            for j, at in enumerate(places):
-                grads_ref[at, :, lo : lo + HEAD] = grad[j * PIECE : (j + 1) * PIECE]
+            grads_ref[:, lo : lo + HEAD] = grad[:PROMPT]
             give_back(grad[PROMPT:], Q_WIDTH + lo)
 
 
-def attention(place, packing, lengths, plan, rows, pieces, slots):
+def attention(place, packing, lengths, rows, prompt):
     flops = 2 * 5 * KEYS * Q_WIDTH // HEAD * SLOTS * HEAD
     block = jax.ShapeDtypeStruct((LOCAL_ROWS, OUT_WIDTH), BF16)
-    part = jax.ShapeDtypeStruct((PLANE * slots, PIECE, 2 * KV_WIDTH), BF16)
-    out = pl.pallas_call(
-        functools.partial(attention_kernel, slots),
-        out_shape=(block,) * N_HEAD + (part,),
-        in_specs=[SMEM] * 4 + [VMEM] * (N_HEAD + 1),
+    *back, grads = pl.pallas_call(
+        attention_kernel,
+        out_shape=(block,) * N_HEAD + (jax.ShapeDtypeStruct((PROMPT, 2 * KV_WIDTH), BF16),),
+        in_specs=[SMEM] * 3 + [VMEM] * (N_HEAD + 1),
         out_specs=(VMEM,) * (N_HEAD + 1),
         scratch_shapes=[
             pltpu.VMEM((KEYS, KV_WIDTH), BF16),
@@ -312,47 +363,49 @@
         cost_estimate=pl.CostEstimate(
             flops=flops, bytes_accessed=6 * 2**20, transcendentals=KEYS * SLOTS * 16
         ),
-    )(place, packing, lengths, plan, *rows, pieces.reshape(part.shape))
-    return out[:N_HEAD], out[N_HEAD].reshape(PLANE, slots * PIECE, 2 * KV_WIDTH)
+    )(place, packing, lengths, *reversed(rows), prompt)
+    return back, grads
 
 
 def exchange(parts, axes):
     return lax.all_to_all(parts, axes, split_axis=0, concat_axis=0, tiled=True)
 
 
-def swap(blocks, which):
-    return [
-        lax.ppermute(block, ("xh", "c"), [(i, i ^ k) for i in range(N_HEAD)])
-        if k in which
-        else block
-        for k, block in enumerate(blocks)
-    ]
+def swap(blocks):
+    blocks = list(blocks)
+    for k in reversed(range(1, N_HEAD)):
+        pairs = [(i, i ^ k) for i in range(N_HEAD)]
+        blocks[k] = lax.ppermute(blocks[k], ("xh", "c"), pairs)
+    return blocks
 
 
 def shards(queries, out_grads, response_kv, prompt_kv, packing, lengths, owner):
     place = jnp.stack([lax.axis_index(("xl", "z", "y")), lax.axis_index(("xh", "c"))])
     place = place.astype(jnp.int32)
     plane = ("xl", "y")
-    others = set(range(1, N_HEAD))
-    line = exchange(spread_piece(prompt_kv), "z")
+    *rows, line = pack(place, queries, out_grads, response_kv, prompt_kv)
+    line = exchange(line, "z")
     plan = make_plan(place, packing, owner)
-    rows = pack_rows(place, queries, out_grads, response_kv)
-    rows = swap(rows, others - set(PLANE_IN))
-
-    def backward(slots, plan, line, *rows):
-        pieces = exchange(select(plan, line, slots), plane)
-        rows = swap(rows, PLANE_IN)
-        back, grads = attention(place, packing, lengths, plan, rows, pieces, slots)
-        grads = exchange(grads, plane)
-        return swap(back, PLANE_OUT), sum_plane(plan, grads, slots)
-
-    back, grads = lax.switch(
-        plan[CHOICE, 0],
-        [functools.partial(backward, slots) for slots in SLOT_COUNTS],
-        plan, line, *rows,
+    rows = swap(rows)
+
+    def gather(slots, line):
+        parts = exchange(select(plan, line, slots), plane)
+        return collect(place, packing, plan, parts, slots)
+
+    def reduce(slots, grads):
+        parts = exchange(scatter(place, packing, plan, grads, slots), plane)
+        return sum_plane(plan, parts, slots)
+
+    choice = plan[CHOICE, 0]
+    prompt = lax.switch(
+        choice, [functools.partial(gather, slots) for slots in SLOT_COUNTS], line
+    )
+    back, grads = attention(place, packing, lengths, rows, prompt)
+    grads = lax.switch(
+        choice, [functools.partial(reduce, slots) for slots in SLOT_COUNTS], grads
     )
     grads = exchange(grads, "z")
-    back = swap(back, others - set(PLANE_OUT))
+    back = swap(back)
     query_grad, resp_grad = unpack_rows(place, back)
     return query_grad, resp_grad, sum_line(grads)
 

time: 114 us -> 97.6 us (0.86)
  the two profiles are of different devices: /device:TPU:2 before, /device:TPU:4 now
where the time goes in v3:
time: 97.6 us; the launch traced here: 96.9 us
  starting transfers between devices  42.3 us (43%)
  blocking collectives  26.2 us (27%)
  Pallas kernels  13.3 us (14%)
  waiting for transfers between devices  13.1 us (13%)
  between operations  1.44 us (1%)
    all_to_all x2, blocking collectives, exchange(): return lax.all_to_all(parts, axes, split_axis=0, concat_axis=0, tiled=True)  26.2 us
    all_to_all x2, starting transfers between devices, exchange(): return lax.all_to_all(parts, axes, split_axis=0, concat_axis=0, tiled=True)  24.1 us
    ppermute x6, starting transfers between devices, swap(): blocks[k] = lax.ppermute(blocks[k], ('xh', 'c'), pairs)  18.2 us
    all_to_all x2, waiting for transfers between devices, exchange(): return lax.all_to_all(parts, axes, split_axis=0, concat_axis=0, tiled=True)  9.9 us
    pallas_call x1, Pallas kernels, attention(): pl.pallas_call(attention_kernel, out_shape=(block,) * N_HEAD + (jax.Shape...  3.95 us
    ppermute x6, waiting for transfers between devices, swap(): blocks[k] = lax.ppermute(blocks[k], ('xh', 'c'), pairs)  3.22 us
    pallas_call x1, Pallas kernels, pack(): pl.pallas_call(pack_kernel, out_shape=(jax.ShapeDtypeStruct((LOCAL_ROWS,...  2.67 us
  transfers between devices with their start and end apart: 8, of which 3 were waited for; matrix products, arithmetic and copies ran while one was open for 1% of the time, Pallas kernels for 4%

profile of v3, /device:TPU:4, one launch (start us, length us, event | category | flops | bytes accessed | tf_op | source)
XLA Modules:
  0.0 96.9 jit_solution(5133930354105324247)
XLA Ops:
  0.6 0.1 pad_add_fusion.place_ref
  0.7 2.7 %shard_map.94 = (bf16[32,4608]{1,0:T(8,128)(2,1)S(1)}, bf16[32,4608]{1,0:T(8,128)(2,1)S(1)}, bf16[32,4608]{1,0:T(8,128)(2,1)S(1)}, bf16[32,4608]{1,0:T(8,128)(2,1)S(1)}, bf16[16,16,512]{2,1,0:T(8,128)(2,1)}) custom-call(s32[2]{0:T(128)S(1)} %pad_add_fusion.place_ref, bf16[32,8192]{1,0:T(8,128)(2,1)} %q_ref.1, bf16[32,8192]{1,0:T(8,128)(2,1)} %g_ref.1, ...), custom_call_target="tpu_custom_call" | custom-call | tf_op jit(solution)/shard_map/pallas_call | solution.py:144
  3.4 15.2 %all-to-all-start.12 = ((bf16[16,16,512]{2,1,0:T(8,128)(2,1)}), bf16[16,16,512]{2,1,0:T(8,128)(2,1)S(1)}, u32[]{:S(2)}, u32[]{:S(2)}) async-start(bf16[16,16,512]{2,1,0:T(8,128)(2,1)} %get-tuple-element.177), calls=%async_computation.12 | async-start | bytes 524288 | tf_op jit(solution)/shard_map/all_to_all | solution.py:371
  18.6 1.9 %collective-permute-start = (bf16[32,4608]{1,0:T(8,128)(2,1)S(1)}, bf16[32,4608]{1,0:T(8,128)(2,1)S(1)}, u32[]{:S(2)}, u32[]{:S(2)}) collective-permute-start(bf16[32,4608]{1,0:T(8,128)(2,1)S(1)} %get-tuple-element.173), channel_id=1, source_target_pairs={{0,3},{1,2},{2,1},{3,0},{4,7},{5,6},{6,5},{7,4},{8,11},{9,10},{10,... | collective-permute-start | bytes 884744 | tf_op jit(solution)/shard_map/ppermute | solution.py:378
  20.5 4.6 %collective-permute-start.1 = (bf16[32,4608]{1,0:T(8,128)(2,1)S(1)}, bf16[32,4608]{1,0:T(8,128)(2,1)S(1)}, u32[]{:S(2)}, u32[]{:S(2)}) collective-permute-start(bf16[32,4608]{1,0:T(8,128)(2,1)S(1)} %get-tuple-element.174), channel_id=1, source_target_pairs={{0,2},{1,3},{2,0},{3,1},{4,6},{5,7},{6,4},{7,5},{8,10},{9,11},{10,... | collective-permute-start | bytes 884744 | tf_op jit(solution)/shard_map/ppermute | solution.py:378
  25.1 2.6 %collective-permute-start.2 = (bf16[32,4608]{1,0:T(8,128)(2,1)S(1)}, bf16[32,4608]{1,0:T(8,128)(2,1)S(1)}, u32[]{:S(2)}, u32[]{:S(2)}) collective-permute-start(bf16[32,4608]{1,0:T(8,128)(2,1)S(1)} %get-tuple-element.175), channel_id=1, source_target_pairs={{0,1},{1,0},{2,3},{3,2},{4,5},{5,4},{6,7},{7,6},{8,9},{9,8},{10,11... | collective-permute-start | bytes 884744 | tf_op jit(solution)/shard_map/ppermute | solution.py:378
  27.7 1.0 shard_map.95
  28.7 0.5 slice.3
  29.8 7.1 %all-to-all-done.12 = bf16[16,16,512]{2,1,0:T(8,128)(2,1)S(1)} async-done(((bf16[16,16,512]{2,1,0:T(8,128)(2,1)}), bf16[16,16,512]{2,1,0:T(8,128)(2,1)S(1)}, u32[]{:S(2)}, u32[]{:S(2)}) %all-to-all-start.12) | async-done | bytes 262176 | tf_op jit(solution)/shard_map/all_to_all | solution.py:371
  37.0 0.0 copy-start
  37.0 15.7 %conditional.2 = (bf16[256,512]{1,0:T(8,128)(2,1)S(1)}) conditional(s32[]{:T(128)} %bitcast.27, (s32[4,128]{1,0:T(4,128)S(1)}, bf16[16,16,512]{2,1,0:T(8,128)(2,1)S(1)}, s32[2]{0:T(128)S(1)}, s32[128]{0:T(128)}) %tuple.44, (s32[4,128]{1,0:T(4,128)S(1)}, bf16[16,16,512]{2,1,0:T(8,128)(2,1)S(1)}, s32[2]{0:T(128)S(1)}, ...), branch_computations={%region_0.0_spmd, %region_1.0_spmd, %region_2.0_spmd, %region_3.0_... | conditional | bytes 4196388 | solution.py:400
  37.0 0.0 copy-start.2
  37.0 0.8 branch_1_fun.4
  37.8 14.2 %all_to_all.59 = bf16[8,80,512]{2,1,0:T(8,128)(2,1)S(1)} all-to-all(bf16[8,80,512]{2,1,0:T(8,128)(2,1)S(1)} %bitcast.46), channel_id=1, replica_groups=mesh['xl'=2,'z'=16,'y'=4,'xh'=2,'c'=2] {'xl','y'}, dimensions={0} | all-to-all | bytes 1310720 | tf_op jit(solution)/shard_map/cond/branch_1_fun/all_to_all | solution.py:371
  52.0 0.0 copy-done.2
  52.0 0.6 branch_1_fun.5
  52.6 0.0 copy-start.1
  52.6 0.0 collective-permute-done.refs_0_
  52.7 0.0 collective-permute-done.1.refs_1_
  52.7 0.0 collective-permute-done.2.refs_2_
  52.7 0.0 copy-done
  52.7 4.0 %shard_map.96 = (bf16[32,2560]{1,0:T(8,128)(2,1)S(1)}, bf16[32,2560]{1,0:T(8,128)(2,1)S(1)}, bf16[32,2560]{1,0:T(8,128)(2,1)S(1)}, bf16[32,2560]{1,0:T(8,128)(2,1)S(1)}, bf16[256,512]{1,0:T(8,128)(2,1)S(1)}) custom-call(s32[2]{0:T(128)S(1)} %pad_add_fusion.place_ref, s32[128]{0:T(128)} %packing_ref.3, s32[128]{0:T(128)S(1)} %copy-done, ...), custom_call_target="tpu_custom_call" | custom-call | flops 1006632960 | bytes 6291456 | tf_op jit(solution)/shard_map/pallas_call | solution.py:351
  56.6 0.0 copy-done.1
  56.7 14.2 %conditional.3 = (bf16[16,16,512]{2,1,0:T(8,128)(2,1)}) conditional(s32[]{:T(128)} %bitcast.27, (s32[2]{0:T(128)S(1)}, s32[128]{0:T(128)S(1)}, s32[4,128]{1,0:T(4,128)S(1)}, bf16[256,512]{1,0:T(8,128)(2,1)S(1)}) %tuple.59, (s32[2]{0:T(128)S(1)}, s32[128]{0:T(128)S(1)}, s32[4,128]{1,0:T(4,128)S(1)}, ...), branch_computations={%region_6.0_spmd, %region_7.0_spmd, %region_8.0_spmd, %region_9.0_... | conditional | bytes 4194312 | solution.py:404
  56.7 0.6 branch_1_fun.6
  57.3 11.9 %all_to_all.65 = bf16[8,80,512]{2,1,0:T(8,128)(2,1)S(1)} all-to-all(bf16[8,80,512]{2,1,0:T(8,128)(2,1)S(1)} %bitcast.47), channel_id=1, replica_groups=mesh['xl'=2,'z'=16,'y'=4,'xh'=2,'c'=2] {'xl','y'}, dimensions={0} | all-to-all | bytes 1310720 | tf_op jit(solution)/shard_map/cond/branch_1_fun/all_to_all | solution.py:371
  69.2 1.6 %branch_1_fun.7 = bf16[16,16,512]{2,1,0:T(8,128)(2,1)} custom-call(s32[4,128]{1,0:T(4,128)S(1)} %get-tuple-element.138.plan_ref, bf16[40,16,512]{2,1,0:T(8,128)(2,1)S(1)} %bitcast.45), custom_call_target="tpu_custom_call" | custom-call | tf_op jit(solution)/shard_map/cond/branch_1_fun/pallas_call | solution.py:234
  70.8 8.9 %all-to-all-start.13 = ((bf16[16,16,512]{2,1,0:T(8,128)(2,1)}), bf16[16,16,512]{2,1,0:T(8,128)(2,1)S(1)}, u32[]{:S(2)}, u32[]{:S(2)}) async-start(bf16[16,16,512]{2,1,0:T(8,128)(2,1)} %get-tuple-element.186), calls=%async_computation.13 | async-start | bytes 524288 | tf_op jit(solution)/shard_map/all_to_all | solution.py:371
  79.7 1.9 %collective-permute-start.3 = (bf16[32,2560]{1,0:T(8,128)(2,1)S(1)}, bf16[32,2560]{1,0:T(8,128)(2,1)S(1)}, u32[]{:S(2)}, u32[]{:S(2)}) collective-permute-start(bf16[32,2560]{1,0:T(8,128)(2,1)S(1)} %get-tuple-element.178), channel_id=1, source_target_pairs={{0,3},{1,2},{2,1},{3,0},{4,7},{5,6},{6,5},{7,4},{8,11},{9,10},{10,... | collective-permute-start | bytes 491528 | tf_op jit(solution)/shard_map/ppermute | solution.py:378
  81.6 2.7 %collective-permute-start.4 = (bf16[32,2560]{1,0:T(8,128)(2,1)S(1)}, bf16[32,2560]{1,0:T(8,128)(2,1)S(1)}, u32[]{:S(2)}, u32[]{:S(2)}) collective-permute-start(bf16[32,2560]{1,0:T(8,128)(2,1)S(1)} %get-tuple-element.179), channel_id=1, source_target_pairs={{0,2},{1,3},{2,0},{3,1},{4,6},{5,7},{6,4},{7,5},{8,10},{9,11},{10,... | collective-permute-start | bytes 491528 | tf_op jit(solution)/shard_map/ppermute | solution.py:378
  84.3 4.5 %collective-permute-start.5 = (bf16[32,2560]{1,0:T(8,128)(2,1)S(1)}, bf16[32,2560]{1,0:T(8,128)(2,1)S(1)}, u32[]{:S(2)}, u32[]{:S(2)}) collective-permute-start(bf16[32,2560]{1,0:T(8,128)(2,1)S(1)} %get-tuple-element.180), channel_id=1, source_target_pairs={{0,1},{1,0},{2,3},{3,2},{4,5},{5,4},{6,7},{7,6},{8,9},{9,8},{10,11... | collective-permute-start | bytes 491528 | tf_op jit(solution)/shard_map/ppermute | solution.py:378
  88.8 0.0 collective-permute-done.3.refs_0_
  88.8 3.2 %collective-permute-done.4.refs_1_ = bf16[32,2560]{1,0:T(8,128)(2,1)S(1)} collective-permute-done((bf16[32,2560]{1,0:T(8,128)(2,1)S(1)}, bf16[32,2560]{1,0:T(8,128)(2,1)S(1)}, u32[]{:S(2)}, u32[]{:S(2)}) %collective-permute-start.4) | collective-permute-done | bytes 163872 | tf_op jit(solution)/shard_map/ppermute | solution.py:378
  92.0 0.0 collective-permute-done.5.refs_2_
  92.0 1.4 %shard_map.97 = (bf16[32,8192]{1,0:T(8,128)(2,1)}, bf16[32,2,1024]{2,1,0:T(2,128)(2,1)}) custom-call(s32[2]{0:T(128)S(1)} %pad_add_fusion.place_ref, bf16[32,2560]{1,0:T(8,128)(2,1)S(1)} %collective-permute-done.3.refs_0_, bf16[32,2560]{1,0:T(8,128)(2,1)S(1)} %collective-permute-done.4.refs_1_, bf16[32,2560]{1,0:T(8,128)(2,1)S(1)} %collective-permute-done.5.refs_2_, ...), custom_call_target="tpu_custom_call" | custom-call | tf_op jit(solution)/shard_map/pallas_call | solution.py:171
  93.5 2.8 %all-to-all-done.13.in_ref = bf16[16,16,512]{2,1,0:T(8,128)(2,1)S(1)} async-done(((bf16[16,16,512]{2,1,0:T(8,128)(2,1)}), bf16[16,16,512]{2,1,0:T(8,128)(2,1)S(1)}, u32[]{:S(2)}, u32[]{:S(2)}) %all-to-all-start.13) | async-done | bytes 262176 | tf_op jit(solution)/shard_map/all_to_all | solution.py:371
  96.3 0.7 shard_map.98
Async XLA Ops:
  3.4 33.6 %all-to-all-start.12 = ((bf16[16,16,512]{2,1,0:T(8,128)(2,1)}), bf16[16,16,512]{2,1,0:T(8,128)(2,1)S(1)}, u32[]{:S(2)}, u32[]{:S(2)}) async-start(bf16[16,16,512]{2,1,0:T(8,128)(2,1)} %get-tuple-element.177), calls=%async_computation.12 | async-start | bytes 524288 | tf_op jit(solution)/shard_map/all_to_all | solution.py:371
  18.6 34.0 %collective-permute-start = (bf16[32,4608]{1,0:T(8,128)(2,1)S(1)}, bf16[32,4608]{1,0:T(8,128)(2,1)S(1)}, u32[]{:S(2)}, u32[]{:S(2)}) collective-permute-start(bf16[32,4608]{1,0:T(8,128)(2,1)S(1)} %get-tuple-element.173), channel_id=1, source_target_pairs={{0,3},{1,2},{2,1},{3,0},{4,7},{5,6},{6,5},{7,4},{8,11},{9,10},{10,... | collective-permute-start | bytes 884744 | tf_op jit(solution)/shard_map/ppermute | solution.py:378
  20.5 32.1 %collective-permute-start.1 = (bf16[32,4608]{1,0:T(8,128)(2,1)S(1)}, bf16[32,4608]{1,0:T(8,128)(2,1)S(1)}, u32[]{:S(2)}, u32[]{:S(2)}) collective-permute-start(bf16[32,4608]{1,0:T(8,128)(2,1)S(1)} %get-tuple-element.174), channel_id=1, source_target_pairs={{0,2},{1,3},{2,0},{3,1},{4,6},{5,7},{6,4},{7,5},{8,10},{9,11},{10,... | collective-permute-start | bytes 884744 | tf_op jit(solution)/shard_map/ppermute | solution.py:378
  25.1 27.5 %collective-permute-start.2 = (bf16[32,4608]{1,0:T(8,128)(2,1)S(1)}, bf16[32,4608]{1,0:T(8,128)(2,1)S(1)}, u32[]{:S(2)}, u32[]{:S(2)}) collective-permute-start(bf16[32,4608]{1,0:T(8,128)(2,1)S(1)} %get-tuple-element.175), channel_id=1, source_target_pairs={{0,1},{1,0},{2,3},{3,2},{4,5},{5,4},{6,7},{7,6},{8,9},{9,8},{10,11... | collective-permute-start | bytes 884744 | tf_op jit(solution)/shard_map/ppermute | solution.py:378
  37.0 15.7 %copy-start = (s32[128]{0:T(128)S(1)}, s32[128]{0:T(128)}, u32[]{:S(2)}) copy-start(s32[128]{0:T(128)} %lengths_ref.1) | copy-start | bytes 1540
  37.0 15.0 %copy-start.2 = (s32[128]{0:T(128)S(1)}, s32[128]{0:T(128)}, u32[]{:S(2)}) copy-start(s32[128]{0:T(128)} %get-tuple-element.110.packing_ref) | copy-start | bytes 1540 | tf_op jit(solution)/shard_map/cond
  52.6 4.0 %copy-start.1 = (s32[128]{0:T(128)S(1)}, s32[128]{0:T(128)}, u32[]{:S(2)}) copy-start(s32[128]{0:T(128)} %packing_ref.3) | copy-start | bytes 1540
  70.8 25.4 %all-to-all-start.13 = ((bf16[16,16,512]{2,1,0:T(8,128)(2,1)}), bf16[16,16,512]{2,1,0:T(8,128)(2,1)S(1)}, u32[]{:S(2)}, u32[]{:S(2)}) async-start(bf16[16,16,512]{2,1,0:T(8,128)(2,1)} %get-tuple-element.186), calls=%async_computation.13 | async-start | bytes 524288 | tf_op jit(solution)/shard_map/all_to_all | solution.py:371
  79.7 9.1 %collective-permute-start.3 = (bf16[32,2560]{1,0:T(8,128)(2,1)S(1)}, bf16[32,2560]{1,0:T(8,128)(2,1)S(1)}, u32[]{:S(2)}, u32[]{:S(2)}) collective-permute-start(bf16[32,2560]{1,0:T(8,128)(2,1)S(1)} %get-tuple-element.178), channel_id=1, source_target_pairs={{0,3},{1,2},{2,1},{3,0},{4,7},{5,6},{6,5},{7,4},{8,11},{9,10},{10,... | collective-permute-start | bytes 491528 | tf_op jit(solution)/shard_map/ppermute | solution.py:378
  81.6 10.4 %collective-permute-start.4 = (bf16[32,2560]{1,0:T(8,128)(2,1)S(1)}, bf16[32,2560]{1,0:T(8,128)(2,1)S(1)}, u32[]{:S(2)}, u32[]{:S(2)}) collective-permute-start(bf16[32,2560]{1,0:T(8,128)(2,1)S(1)} %get-tuple-element.179), channel_id=1, source_target_pairs={{0,2},{1,3},{2,0},{3,1},{4,6},{5,7},{6,4},{7,5},{8,10},{9,11},{10,... | collective-permute-start | bytes 491528 | tf_op jit(solution)/shard_map/ppermute | solution.py:378
  84.3 7.7 %collective-permute-start.5 = (bf16[32,2560]{1,0:T(8,128)(2,1)S(1)}, bf16[32,2560]{1,0:T(8,128)(2,1)S(1)}, u32[]{:S(2)}, u32[]{:S(2)}) collective-permute-start(bf16[32,2560]{1,0:T(8,128)(2,1)S(1)} %get-tuple-element.180), channel_id=1, source_target_pairs={{0,1},{1,0},{2,3},{3,2},{4,5},{5,4},{6,7},{7,6},{8,9},{9,8},{10,11... | collective-permute-start | bytes 491528 | tf_op jit(solution)/shard_map/ppermute | solution.py:378

commit v4 on v3

--- a/solution.py
+++ b/solution.py
@@ -112,24 +112,27 @@
     return out.reshape(PLANE, slots * PIECE, 2 * KV_WIDTH)
 
 
-def pack_kernel(place_ref, q_ref, g_ref, kv_ref, piece_ref, *refs):
-    row_refs, line_ref, kv_here, piece_here, sems = refs[:N_HEAD], *refs[N_HEAD:]
+def pack_kernel(q_ref, g_ref, kv_ref, piece_ref, *refs):
+    row_refs, line_ref, kv_here, piece_here, line_here, sems = refs[:N_HEAD], *refs[N_HEAD:]
     fetch_piece = pltpu.make_async_copy(piece_ref, piece_here, sems.at[0])
     fetch_kv = pltpu.make_async_copy(kv_ref, kv_here, sems.at[1])
+    store_line = pltpu.make_async_copy(line_here, line_ref, sems.at[2])
     fetch_piece.start()
     fetch_kv.start()
-    others = [place_ref[1] ^ k for k in range(N_HEAD)]
+    head = lax.axis_index("xh") * 2 + lax.axis_index("c")
+    others = [head ^ k for k in range(N_HEAD)]
     fetches = []
-    for k, (other, out_ref) in enumerate(zip(others, row_refs)):
-        wide = pl.ds(pl.multiple_of(other * Q_WIDTH, Q_WIDTH), Q_WIDTH)
+    for k in reversed(range(N_HEAD)):
+        wide = pl.ds(pl.multiple_of(others[k] * Q_WIDTH, Q_WIDTH), Q_WIDTH)
         for i, ref in enumerate((q_ref, g_ref)):
-            here = out_ref.at[:, i * Q_WIDTH : (i + 1) * Q_WIDTH]
-            fetches.append(pltpu.make_async_copy(ref.at[:, wide], here, sems.at[2 + 2 * k + i]))
+            here = row_refs[k].at[:, i * Q_WIDTH : (i + 1) * Q_WIDTH]
+            fetches.append(pltpu.make_async_copy(ref.at[:, wide], here, sems.at[3 + 2 * k + i]))
             fetches[-1].start()
     fetch_piece.wait()
     flat = jnp.concatenate([piece_here[:, 0, :], piece_here[:, 1, :]], axis=1)
     for z in range(Z):
-        line_ref[z] = flat
+        line_here[z] = flat
+    store_line.start()
     fetch_kv.wait()
     for other, out_ref in zip(others, row_refs):
         narrow = pl.ds(pl.multiple_of(other * KV_WIDTH, KV_WIDTH), KV_WIDTH)
@@ -138,22 +141,26 @@
             out_ref[:, lo : lo + KV_WIDTH] = kv_here[:, i, narrow]
     for fetch in fetches:
         fetch.wait()
-
-
-def pack(place, queries, grads, kv, piece):
+    store_line.wait()
+
+
+def pack(queries, grads, kv, piece):
+    args = [pltpu.with_memory_space_constraint(x, pltpu.HBM) for x in (queries, grads, kv, piece)]
+    line = jax.ShapeDtypeStruct((Z, PIECE, 2 * KV_WIDTH), BF16)
+    hbm = pl.BlockSpec(memory_space=pltpu.HBM)
     return pl.pallas_call(
         pack_kernel,
-        out_shape=(jax.ShapeDtypeStruct((LOCAL_ROWS, IN_WIDTH), BF16),) * N_HEAD
-        + (jax.ShapeDtypeStruct((Z, PIECE, 2 * KV_WIDTH), BF16),),
-        in_specs=[SMEM] + [pl.BlockSpec(memory_space=pltpu.HBM)] * 4,
-        out_specs=(VMEM,) * (N_HEAD + 1),
+        out_shape=(jax.ShapeDtypeStruct((LOCAL_ROWS, IN_WIDTH), BF16),) * N_HEAD + (line,),
+        in_specs=[hbm] * 4,
+        out_specs=(VMEM,) * N_HEAD + (hbm,),
         scratch_shapes=[
             pltpu.VMEM(kv.shape, BF16),
             pltpu.VMEM(piece.shape, BF16),
-            pltpu.SemaphoreType.DMA((2 + 2 * N_HEAD,)),
+            pltpu.VMEM(line.shape, BF16),
+            pltpu.SemaphoreType.DMA((3 + 2 * N_HEAD,)),
         ],
         compiler_params=params(16),
-    )(place, *[pltpu.with_memory_space_constraint(x, pltpu.HBM) for x in (queries, grads, kv, piece)])
+    )(*args)
 
 
 def unpack_kernel(place_ref, *refs):
@@ -383,7 +390,7 @@
     place = jnp.stack([lax.axis_index(("xl", "z", "y")), lax.axis_index(("xh", "c"))])
     place = place.astype(jnp.int32)
     plane = ("xl", "y")
-    *rows, line = pack(place, queries, out_grads, response_kv, prompt_kv)
+    *rows, line = pack(queries, out_grads, response_kv, prompt_kv)
     line = exchange(line, "z")
     plan = make_plan(place, packing, owner)
     rows = swap(rows)

time: 97.6 us -> 97.5 us (level)
  blocking collectives: 26.2 us -> 27.6 us
  Pallas kernels: 13.3 us -> 12.2 us
  starting transfers between devices: 42.3 us -> 43.4 us
    all_to_all x2, blocking collectives: 26.2 us -> 27.6 us  [exchange(): return lax.all_to_all(parts, axes, split_axis=0, concat_axis=0, tiled=True)]
    all_to_all x2, starting transfers between devices: 24.1 us -> 25.2 us  [exchange(): return lax.all_to_all(parts, axes, split_axis=0, concat_axis=0, tiled=True)]
    pallas_call x1, Pallas kernels: 2.67 us -> 1.57 us  [pack(): pl.pallas_call(pack_kernel, out_shape=(jax.ShapeDtypeStruct((LOCAL_ROWS,...]
where the time goes in v4:
time: 97.5 us; the launch traced here: 97.7 us
  starting transfers between devices  43.4 us (45%)
  blocking collectives  27.6 us (28%)
  waiting for transfers between devices  12.4 us (13%)
  Pallas kernels  12.2 us (13%)
  between operations  1.44 us (1%)
    all_to_all x2, blocking collectives, exchange(): return lax.all_to_all(parts, axes, split_axis=0, concat_axis=0, tiled=True)  27.6 us
    all_to_all x2, starting transfers between devices, exchange(): return lax.all_to_all(parts, axes, split_axis=0, concat_axis=0, tiled=True)  25.2 us
    ppermute x6, starting transfers between devices, swap(): blocks[k] = lax.ppermute(blocks[k], ('xh', 'c'), pairs)  18.2 us
    all_to_all x2, waiting for transfers between devices, exchange(): return lax.all_to_all(parts, axes, split_axis=0, concat_axis=0, tiled=True)  9.19 us
    pallas_call x1, Pallas kernels, attention(): pl.pallas_call(attention_kernel, out_shape=(block,) * N_HEAD + (jax.Shape...  3.94 us
    ppermute x6, waiting for transfers between devices, swap(): blocks[k] = lax.ppermute(blocks[k], ('xh', 'c'), pairs)  3.22 us
  transfers between devices with their start and end apart: 8, of which 3 were waited for; matrix products, arithmetic and copies ran while one was open for 1% of the time, Pallas kernels for 4%

profile of v4, /device:TPU:4, one launch (start us, length us, event | category | flops | bytes accessed | tf_op | source)
XLA Modules:
  0.0 97.7 jit_solution(11135268445507876800)
XLA Ops:
  0.6 1.6 %shard_map.94 = (bf16[32,4608]{1,0:T(8,128)(2,1)S(1)}, bf16[32,4608]{1,0:T(8,128)(2,1)S(1)}, bf16[32,4608]{1,0:T(8,128)(2,1)S(1)}, bf16[32,4608]{1,0:T(8,128)(2,1)S(1)}, bf16[16,16,512]{2,1,0:T(8,128)(2,1)}) custom-call(bf16[32,8192]{1,0:T(8,128)(2,1)} %q_ref.1, bf16[32,8192]{1,0:T(8,128)(2,1)} %g_ref.1, bf16[32,2,1024]{2,1,0:T(2,128)(2,1)} %kv_ref.1, ...), custom_call_target="tpu_custom_call" | custom-call | tf_op jit(solution)/shard_map/pallas_call | solution.py:151
  2.2 15.2 %all-to-all-start.12 = ((bf16[16,16,512]{2,1,0:T(8,128)(2,1)}), bf16[16,16,512]{2,1,0:T(8,128)(2,1)S(1)}, u32[]{:S(2)}, u32[]{:S(2)}) async-start(bf16[16,16,512]{2,1,0:T(8,128)(2,1)} %get-tuple-element.177), calls=%async_computation.12 | async-start | bytes 524288 | tf_op jit(solution)/shard_map/all_to_all | solution.py:378
  17.4 1.9 %collective-permute-start = (bf16[32,4608]{1,0:T(8,128)(2,1)S(1)}, bf16[32,4608]{1,0:T(8,128)(2,1)S(1)}, u32[]{:S(2)}, u32[]{:S(2)}) collective-permute-start(bf16[32,4608]{1,0:T(8,128)(2,1)S(1)} %get-tuple-element.173), channel_id=1, source_target_pairs={{0,3},{1,2},{2,1},{3,0},{4,7},{5,6},{6,5},{7,4},{8,11},{9,10},{10,... | collective-permute-start | bytes 884744 | tf_op jit(solution)/shard_map/ppermute | solution.py:385
  19.4 4.6 %collective-permute-start.1 = (bf16[32,4608]{1,0:T(8,128)(2,1)S(1)}, bf16[32,4608]{1,0:T(8,128)(2,1)S(1)}, u32[]{:S(2)}, u32[]{:S(2)}) collective-permute-start(bf16[32,4608]{1,0:T(8,128)(2,1)S(1)} %get-tuple-element.174), channel_id=1, source_target_pairs={{0,2},{1,3},{2,0},{3,1},{4,6},{5,7},{6,4},{7,5},{8,10},{9,11},{10,... | collective-permute-start | bytes 884744 | tf_op jit(solution)/shard_map/ppermute | solution.py:385
  23.9 2.6 %collective-permute-start.2 = (bf16[32,4608]{1,0:T(8,128)(2,1)S(1)}, bf16[32,4608]{1,0:T(8,128)(2,1)S(1)}, u32[]{:S(2)}, u32[]{:S(2)}) collective-permute-start(bf16[32,4608]{1,0:T(8,128)(2,1)S(1)} %get-tuple-element.175), channel_id=1, source_target_pairs={{0,1},{1,0},{2,3},{3,2},{4,5},{5,4},{6,7},{7,6},{8,9},{9,8},{10,11... | collective-permute-start | bytes 884744 | tf_op jit(solution)/shard_map/ppermute | solution.py:385
  26.5 0.1 pad_add_fusion.place_ref
  26.6 0.9 shard_map.95
  27.6 0.5 slice.3
  28.7 7.0 %all-to-all-done.12 = bf16[16,16,512]{2,1,0:T(8,128)(2,1)S(1)} async-done(((bf16[16,16,512]{2,1,0:T(8,128)(2,1)}), bf16[16,16,512]{2,1,0:T(8,128)(2,1)S(1)}, u32[]{:S(2)}, u32[]{:S(2)}) %all-to-all-start.12) | async-done | bytes 262176 | tf_op jit(solution)/shard_map/all_to_all | solution.py:378
  35.8 0.0 copy-start
  35.8 16.4 %conditional.2 = (bf16[256,512]{1,0:T(8,128)(2,1)S(1)}) conditional(s32[]{:T(128)} %bitcast.27, (s32[4,128]{1,0:T(4,128)S(1)}, bf16[16,16,512]{2,1,0:T(8,128)(2,1)S(1)}, s32[2]{0:T(128)S(1)}, s32[128]{0:T(128)}) %tuple.44, (s32[4,128]{1,0:T(4,128)S(1)}, bf16[16,16,512]{2,1,0:T(8,128)(2,1)S(1)}, s32[2]{0:T(128)S(1)}, ...), branch_computations={%region_0.0_spmd, %region_1.0_spmd, %region_2.0_spmd, %region_3.0_... | conditional | bytes 4196388 | solution.py:407
  35.8 0.0 copy-start.3
  35.8 0.8 branch_2_fun.4
  36.6 14.9 %all_to_all.60 = bf16[8,96,512]{2,1,0:T(8,128)(2,1)S(1)} all-to-all(bf16[8,96,512]{2,1,0:T(8,128)(2,1)S(1)} %bitcast.42), channel_id=1, replica_groups=mesh['xl'=2,'z'=16,'y'=4,'xh'=2,'c'=2] {'xl','y'}, dimensions={0} | all-to-all | bytes 1572864 | tf_op jit(solution)/shard_map/cond/branch_2_fun/all_to_all | solution.py:378
  51.5 0.0 copy-done.3
  51.5 0.6 branch_2_fun.5
  52.1 0.0 copy-start.1
  52.2 0.0 collective-permute-done.refs_0_
  52.2 0.0 collective-permute-done.1.refs_1_
  52.2 0.0 collective-permute-done.2.refs_2_
  52.2 0.0 copy-done
  52.2 3.9 %shard_map.96 = (bf16[32,2560]{1,0:T(8,128)(2,1)S(1)}, bf16[32,2560]{1,0:T(8,128)(2,1)S(1)}, bf16[32,2560]{1,0:T(8,128)(2,1)S(1)}, bf16[32,2560]{1,0:T(8,128)(2,1)S(1)}, bf16[256,512]{1,0:T(8,128)(2,1)S(1)}) custom-call(s32[2]{0:T(128)S(1)} %pad_add_fusion.place_ref, s32[128]{0:T(128)} %packing_ref.3, s32[128]{0:T(128)S(1)} %copy-done, ...), custom_call_target="tpu_custom_call" | custom-call | flops 1006632960 | bytes 6291456 | tf_op jit(solution)/shard_map/pallas_call | solution.py:358
  56.1 0.0 copy-done.1
  56.2 14.9 %conditional.3 = (bf16[16,16,512]{2,1,0:T(8,128)(2,1)}) conditional(s32[]{:T(128)} %bitcast.27, (s32[2]{0:T(128)S(1)}, s32[128]{0:T(128)S(1)}, s32[4,128]{1,0:T(4,128)S(1)}, bf16[256,512]{1,0:T(8,128)(2,1)S(1)}) %tuple.59, (s32[2]{0:T(128)S(1)}, s32[128]{0:T(128)S(1)}, s32[4,128]{1,0:T(4,128)S(1)}, ...), branch_computations={%region_6.0_spmd, %region_7.0_spmd, %region_8.0_spmd, %region_9.0_... | conditional | bytes 4194312 | solution.py:411
  56.2 0.6 branch_2_fun.6
  56.8 12.6 %all_to_all.66 = bf16[8,96,512]{2,1,0:T(8,128)(2,1)S(1)} all-to-all(bf16[8,96,512]{2,1,0:T(8,128)(2,1)S(1)} %bitcast.43), channel_id=1, replica_groups=mesh['xl'=2,'z'=16,'y'=4,'xh'=2,'c'=2] {'xl','y'}, dimensions={0} | all-to-all | bytes 1572864 | tf_op jit(solution)/shard_map/cond/branch_2_fun/all_to_all | solution.py:378
  69.5 1.6 %branch_2_fun.7 = bf16[16,16,512]{2,1,0:T(8,128)(2,1)} custom-call(s32[4,128]{1,0:T(4,128)S(1)} %get-tuple-element.142.plan_ref, bf16[48,16,512]{2,1,0:T(8,128)(2,1)S(1)} %bitcast.41), custom_call_target="tpu_custom_call" | custom-call | tf_op jit(solution)/shard_map/cond/branch_2_fun/pallas_call | solution.py:241
  71.1 10.0 %all-to-all-start.13 = ((bf16[16,16,512]{2,1,0:T(8,128)(2,1)}), bf16[16,16,512]{2,1,0:T(8,128)(2,1)S(1)}, u32[]{:S(2)}, u32[]{:S(2)}) async-start(bf16[16,16,512]{2,1,0:T(8,128)(2,1)} %get-tuple-element.186), calls=%async_computation.13 | async-start | bytes 524288 | tf_op jit(solution)/shard_map/all_to_all | solution.py:378
  81.1 1.9 %collective-permute-start.3 = (bf16[32,2560]{1,0:T(8,128)(2,1)S(1)}, bf16[32,2560]{1,0:T(8,128)(2,1)S(1)}, u32[]{:S(2)}, u32[]{:S(2)}) collective-permute-start(bf16[32,2560]{1,0:T(8,128)(2,1)S(1)} %get-tuple-element.178), channel_id=1, source_target_pairs={{0,3},{1,2},{2,1},{3,0},{4,7},{5,6},{6,5},{7,4},{8,11},{9,10},{10,... | collective-permute-start | bytes 491528 | tf_op jit(solution)/shard_map/ppermute | solution.py:385
  83.0 2.7 %collective-permute-start.4 = (bf16[32,2560]{1,0:T(8,128)(2,1)S(1)}, bf16[32,2560]{1,0:T(8,128)(2,1)S(1)}, u32[]{:S(2)}, u32[]{:S(2)}) collective-permute-start(bf16[32,2560]{1,0:T(8,128)(2,1)S(1)} %get-tuple-element.179), channel_id=1, source_target_pairs={{0,2},{1,3},{2,0},{3,1},{4,6},{5,7},{6,4},{7,5},{8,10},{9,11},{10,... | collective-permute-start | bytes 491528 | tf_op jit(solution)/shard_map/ppermute | solution.py:385
  85.7 4.5 %collective-permute-start.5 = (bf16[32,2560]{1,0:T(8,128)(2,1)S(1)}, bf16[32,2560]{1,0:T(8,128)(2,1)S(1)}, u32[]{:S(2)}, u32[]{:S(2)}) collective-permute-start(bf16[32,2560]{1,0:T(8,128)(2,1)S(1)} %get-tuple-element.180), channel_id=1, source_target_pairs={{0,1},{1,0},{2,3},{3,2},{4,5},{5,4},{6,7},{7,6},{8,9},{9,8},{10,11... | collective-permute-start | bytes 491528 | tf_op jit(solution)/shard_map/ppermute | solution.py:385
  90.2 0.0 collective-permute-done.3.refs_0_
  90.2 3.2 %collective-permute-done.4.refs_1_ = bf16[32,2560]{1,0:T(8,128)(2,1)S(1)} collective-permute-done((bf16[32,2560]{1,0:T(8,128)(2,1)S(1)}, bf16[32,2560]{1,0:T(8,128)(2,1)S(1)}, u32[]{:S(2)}, u32[]{:S(2)}) %collective-permute-start.4) | collective-permute-done | bytes 163872 | tf_op jit(solution)/shard_map/ppermute | solution.py:385
  93.4 0.0 collective-permute-done.5.refs_2_
  93.4 1.4 %shard_map.97 = (bf16[32,8192]{1,0:T(8,128)(2,1)}, bf16[32,2,1024]{2,1,0:T(2,128)(2,1)}) custom-call(s32[2]{0:T(128)S(1)} %pad_add_fusion.place_ref, bf16[32,2560]{1,0:T(8,128)(2,1)S(1)} %collective-permute-done.3.refs_0_, bf16[32,2560]{1,0:T(8,128)(2,1)S(1)} %collective-permute-done.4.refs_1_, bf16[32,2560]{1,0:T(8,128)(2,1)S(1)} %collective-permute-done.5.refs_2_, ...), custom_call_target="tpu_custom_call" | custom-call | tf_op jit(solution)/shard_map/pallas_call | solution.py:178
  94.9 2.2 %all-to-all-done.13.in_ref = bf16[16,16,512]{2,1,0:T(8,128)(2,1)S(1)} async-done(((bf16[16,16,512]{2,1,0:T(8,128)(2,1)}), bf16[16,16,512]{2,1,0:T(8,128)(2,1)S(1)}, u32[]{:S(2)}, u32[]{:S(2)}) %all-to-all-start.13) | async-done | bytes 262176 | tf_op jit(solution)/shard_map/all_to_all | solution.py:378
  97.0 0.7 shard_map.98
Async XLA Ops:
  2.2 33.6 %all-to-all-start.12 = ((bf16[16,16,512]{2,1,0:T(8,128)(2,1)}), bf16[16,16,512]{2,1,0:T(8,128)(2,1)S(1)}, u32[]{:S(2)}, u32[]{:S(2)}) async-start(bf16[16,16,512]{2,1,0:T(8,128)(2,1)} %get-tuple-element.177), calls=%async_computation.12 | async-start | bytes 524288 | tf_op jit(solution)/shard_map/all_to_all | solution.py:378
  17.4 34.7 %collective-permute-start = (bf16[32,4608]{1,0:T(8,128)(2,1)S(1)}, bf16[32,4608]{1,0:T(8,128)(2,1)S(1)}, u32[]{:S(2)}, u32[]{:S(2)}) collective-permute-start(bf16[32,4608]{1,0:T(8,128)(2,1)S(1)} %get-tuple-element.173), channel_id=1, source_target_pairs={{0,3},{1,2},{2,1},{3,0},{4,7},{5,6},{6,5},{7,4},{8,11},{9,10},{10,... | collective-permute-start | bytes 884744 | tf_op jit(solution)/shard_map/ppermute | solution.py:385
  19.4 32.8 %collective-permute-start.1 = (bf16[32,4608]{1,0:T(8,128)(2,1)S(1)}, bf16[32,4608]{1,0:T(8,128)(2,1)S(1)}, u32[]{:S(2)}, u32[]{:S(2)}) collective-permute-start(bf16[32,4608]{1,0:T(8,128)(2,1)S(1)} %get-tuple-element.174), channel_id=1, source_target_pairs={{0,2},{1,3},{2,0},{3,1},{4,6},{5,7},{6,4},{7,5},{8,10},{9,11},{10,... | collective-permute-start | bytes 884744 | tf_op jit(solution)/shard_map/ppermute | solution.py:385
  23.9 28.2 %collective-permute-start.2 = (bf16[32,4608]{1,0:T(8,128)(2,1)S(1)}, bf16[32,4608]{1,0:T(8,128)(2,1)S(1)}, u32[]{:S(2)}, u32[]{:S(2)}) collective-permute-start(bf16[32,4608]{1,0:T(8,128)(2,1)S(1)} %get-tuple-element.175), channel_id=1, source_target_pairs={{0,1},{1,0},{2,3},{3,2},{4,5},{5,4},{6,7},{7,6},{8,9},{9,8},{10,11... | collective-permute-start | bytes 884744 | tf_op jit(solution)/shard_map/ppermute | solution.py:385
  35.8 16.4 %copy-start = (s32[128]{0:T(128)S(1)}, s32[128]{0:T(128)}, u32[]{:S(2)}) copy-start(s32[128]{0:T(128)} %lengths_ref.1) | copy-start | bytes 1540
  35.8 15.7 %copy-start.3 = (s32[128]{0:T(128)S(1)}, s32[128]{0:T(128)}, u32[]{:S(2)}) copy-start(s32[128]{0:T(128)} %get-tuple-element.114.packing_ref) | copy-start | bytes 1540 | tf_op jit(solution)/shard_map/cond
  52.1 4.0 %copy-start.1 = (s32[128]{0:T(128)S(1)}, s32[128]{0:T(128)}, u32[]{:S(2)}) copy-start(s32[128]{0:T(128)} %packing_ref.3) | copy-start | bytes 1540
  71.1 26.0 %all-to-all-start.13 = ((bf16[16,16,512]{2,1,0:T(8,128)(2,1)}), bf16[16,16,512]{2,1,0:T(8,128)(2,1)S(1)}, u32[]{:S(2)}, u32[]{:S(2)}) async-start(bf16[16,16,512]{2,1,0:T(8,128)(2,1)} %get-tuple-element.186), calls=%async_computation.13 | async-start | bytes 524288 | tf_op jit(solution)/shard_map/all_to_all | solution.py:378
  81.1 9.1 %collective-permute-start.3 = (bf16[32,2560]{1,0:T(8,128)(2,1)S(1)}, bf16[32,2560]{1,0:T(8,128)(2,1)S(1)}, u32[]{:S(2)}, u32[]{:S(2)}) collective-permute-start(bf16[32,2560]{1,0:T(8,128)(2,1)S(1)} %get-tuple-element.178), channel_id=1, source_target_pairs={{0,3},{1,2},{2,1},{3,0},{4,7},{5,6},{6,5},{7,4},{8,11},{9,10},{10,... | collective-permute-start | bytes 491528 | tf_op jit(solution)/shard_map/ppermute | solution.py:385
  83.0 10.4 %collective-permute-start.4 = (bf16[32,2560]{1,0:T(8,128)(2,1)S(1)}, bf16[32,2560]{1,0:T(8,128)(2,1)S(1)}, u32[]{:S(2)}, u32[]{:S(2)}) collective-permute-start(bf16[32,2560]{1,0:T(8,128)(2,1)S(1)} %get-tuple-element.179), channel_id=1, source_target_pairs={{0,2},{1,3},{2,0},{3,1},{4,6},{5,7},{6,4},{7,5},{8,10},{9,11},{10,... | collective-permute-start | bytes 491528 | tf_op jit(solution)/shard_map/ppermute | solution.py:385
  85.7 7.7 %collective-permute-start.5 = (bf16[32,2560]{1,0:T(8,128)(2,1)S(1)}, bf16[32,2560]{1,0:T(8,128)(2,1)S(1)}, u32[]{:S(2)}, u32[]{:S(2)}) collective-permute-start(bf16[32,2560]{1,0:T(8,128)(2,1)S(1)} %get-tuple-element.180), channel_id=1, source_target_pairs={{0,1},{1,0},{2,3},{3,2},{4,5},{5,4},{6,7},{7,6},{8,9},{9,8},{10,11... | collective-permute-start | bytes 491528 | tf_op jit(solution)/shard_map/ppermute | solution.py:385

commit v5 on v4

--- a/solution.py
+++ b/solution.py
@@ -29,7 +29,7 @@
 KV_WIDTH = KV_LOCAL * HEAD
 IN_WIDTH = 2 * Q_WIDTH + 2 * KV_WIDTH
 OUT_WIDTH = Q_WIDTH + 2 * KV_WIDTH
-CHUNK, STRIP = 8, 64
+CHUNK, STRIP, AHEAD, BEHIND = 8, 64, 1, 0
 INV_ROOT = 1.0 / math.sqrt(HEAD)
 EXP2_SCALE = INV_ROOT / math.log(2.0)
 
@@ -208,22 +208,6 @@
     )(place, packing, plan, parts.reshape(PLANE * slots, PIECE, 2 * KV_WIDTH))
 
 
-def scatter_kernel(slots, place_ref, packing_ref, plan_ref, rows_ref, out_ref):
-    for j, at in enumerate(slots_of(place_ref, packing_ref, plan_ref, slots)):
-        out_ref[at] = rows_ref[j * PIECE : (j + 1) * PIECE]
-
-
-def scatter(place, packing, plan, rows, slots):
-    out = pl.pallas_call(
-        functools.partial(scatter_kernel, slots),
-        out_shape=jax.ShapeDtypeStruct((PLANE * slots, PIECE, 2 * KV_WIDTH), BF16),
-        in_specs=[SMEM, SMEM, SMEM, VMEM],
-        out_specs=VMEM,
-        compiler_params=params(16),
-    )(place, packing, plan, rows)
-    return out.reshape(PLANE, slots * PIECE, 2 * KV_WIDTH)
-
-
 def sum_plane_kernel(slots, plan_ref, part_ref, out_ref, total_ref):
     total_ref[...] = jnp.zeros_like(total_ref)
     for d in range(PLANE):
@@ -271,7 +255,7 @@
     return ((row // LOCAL_ROWS) ^ head) * LOCAL_ROWS + row % LOCAL_ROWS
 
 
-def attention_kernel(place_ref, packing_ref, lengths_ref, *refs):
+def attention_kernel(slots, place_ref, packing_ref, lengths_ref, plan_ref, *refs):
     row_refs, prompt_ref, refs = refs[N_HEAD - 1 :: -1], refs[N_HEAD], refs[N_HEAD + 1 :]
     back_refs, grads_ref, refs = refs[:N_HEAD], refs[N_HEAD], refs[N_HEAD + 1 :]
     key_ref, value_ref, weight_ref, dscore_ref = refs
@@ -284,6 +268,7 @@
             ref[:, lo : lo + HEAD] = block[k * LOCAL_ROWS : (k + 1) * LOCAL_ROWS]
 
     length = lengths_ref[packing_ref[place_ref[0]]]
+    places = slots_of(place_ref, packing_ref, plan_ref, slots)
     key_ref[:PROMPT] = prompt_ref[:, :KV_WIDTH]
     value_ref[:PROMPT] = prompt_ref[:, KV_WIDTH:]
     for g in range(KV_LOCAL):
@@ -300,78 +285,103 @@
     def fold(x):
         return jnp.sum(x.reshape(STRIP // 8, 8, width), axis=0)
 
-    for g in range(KV_LOCAL):
+    def products(g, c):
         cols = slice(g * HEAD, (g + 1) * HEAD)
-        keys, values = key_ref[:, cols], value_ref[:, cols]
-        keys_down = keys.T
-        queries, out_grads = [], []
-        for c in range(PER_GROUP // CHUNK):
-            at = [(g * PER_GROUP + c * CHUNK + i) * HEAD for i in range(CHUNK)]
-            query = jnp.concatenate([rows_of(lo) for lo in at], axis=0)
-            out_grad = jnp.concatenate([rows_of(Q_WIDTH + lo) for lo in at], axis=0)
-            queries.append(query)
-            out_grads.append(out_grad)
-            score = dot(keys, query, ((1,), (1,)))
-            dprob = dot(values, out_grad, ((1,), (1,)))
-            top = None
-            scores = []
-            for strip in strips:
-                part = score[strip]
-                if strip.start >= PROMPT:
-                    key_pos = slot_index((STRIP, 1), 0, head, strip.start - PROMPT)
-                    part = jnp.where(key_pos <= query_pos, part, -jnp.inf)
-                scores.append(part)
-                most = jnp.max(part.reshape(STRIP // 8, 8, width), axis=0)
-                top = most if top is None else jnp.maximum(top, most)
-            shift = jnp.max(top, axis=0, keepdims=True) * EXP2_SCALE
-            raised, total, moment = [], 0.0, 0.0
-            for strip, part in zip(strips, scores):
-                part = jnp.exp2(part * EXP2_SCALE - shift)
-                raised.append(part)
-                total += fold(part)
-                moment += fold(part * dprob[strip])
-            total = jnp.sum(total, axis=0, keepdims=True)
-            moment = jnp.sum(moment, axis=0, keepdims=True)
-            scale = jnp.where(used, 1.0 / total, 0.0)
-            delta = moment * scale
-            here = slice(c * width, (c + 1) * width)
-            for strip, part in zip(strips, raised):
-                weight = part * scale
-                weight_ref[strip, here] = weight.astype(BF16)
-                dscore_ref[strip, here] = (weight * (dprob[strip] - delta)).astype(BF16)
-            query_grad = dot(keys_down, dscore_ref[:, here], ((1,), (0,)))
-            query_grad = (query_grad * INV_ROOT).astype(BF16).T
-            for i, lo in enumerate(at):
-                give_back(query_grad[i * SLOTS : (i + 1) * SLOTS], lo)
-        key_grad = dot(dscore_ref[...], jnp.concatenate(queries, axis=0), ((1,), (0,))) * INV_ROOT
-        value_grad = dot(weight_ref[...], jnp.concatenate(out_grads, axis=0), ((1,), (0,)))
+        at = [(g * PER_GROUP + c * CHUNK + i) * HEAD for i in range(CHUNK)]
+        query = jnp.concatenate([rows_of(lo) for lo in at], axis=0)
+        out_grad = jnp.concatenate([rows_of(Q_WIDTH + lo) for lo in at], axis=0)
+        score = dot(key_ref[:, cols], query, ((1,), (1,)))
+        dprob = dot(value_ref[:, cols], out_grad, ((1,), (1,)))
+        return query, out_grad, score, dprob
+
+    def softmax(g, c, score, dprob):
+        top, scores = None, []
+        for strip in strips:
+            part = score[strip]
+            if strip.start >= PROMPT:
+                key_pos = slot_index((STRIP, 1), 0, head, strip.start - PROMPT)
+                part = jnp.where(key_pos <= query_pos, part, -jnp.inf)
+            scores.append(part)
+            most = jnp.max(part.reshape(STRIP // 8, 8, width), axis=0)
+            top = most if top is None else jnp.maximum(top, most)
+        shift = jnp.max(top, axis=0, keepdims=True) * EXP2_SCALE
+        raised, total, moment = [], 0.0, 0.0
+        for strip, part in zip(strips, scores):
+            part = jnp.exp2(part * EXP2_SCALE - shift)
+            raised.append(part)
+            total += fold(part)
+            moment += fold(part * dprob[strip])
+        total = jnp.sum(total, axis=0, keepdims=True)
+        moment = jnp.sum(moment, axis=0, keepdims=True)
+        scale = jnp.where(used, 1.0 / total, 0.0)
+        delta = moment * scale
+        here = slice(c * width, (c + 1) * width)
+        for strip, part in zip(strips, raised):
+            weight = part * scale
+            weight_ref[g, strip, here] = weight.astype(BF16)
+            dscore_ref[g, strip, here] = (weight * (dprob[strip] - delta)).astype(BF16)
+
+    def query_side(g, c):
+        keys_down = key_ref[:, g * HEAD : (g + 1) * HEAD].T
+        grad = dot(keys_down, dscore_ref[g, :, c * width : (c + 1) * width], ((1,), (0,)))
+        grad = (grad * INV_ROOT).astype(BF16).T
+        for i in range(CHUNK):
+            give_back(grad[i * SLOTS : (i + 1) * SLOTS], (g * PER_GROUP + c * CHUNK + i) * HEAD)
+
+    def key_side(g, queries, out_grads):
+        key_grad = dot(dscore_ref[g], jnp.concatenate(queries, axis=0), ((1,), (0,))) * INV_ROOT
+        value_grad = dot(weight_ref[g], jnp.concatenate(out_grads, axis=0), ((1,), (0,)))
         for slot, grad in enumerate((key_grad, value_grad)):
             grad = grad.astype(BF16)
             lo = slot * KV_WIDTH + g * HEAD
-            grads_ref[:, lo : lo + HEAD] = grad[:PROMPT]
+            for j, at in enumerate(places):
+                grads_ref[at, :, lo : lo + HEAD] = grad[j * PIECE : (j + 1) * PIECE]
             give_back(grad[PROMPT:], Q_WIDTH + lo)
 
-
-def attention(place, packing, lengths, rows, prompt):
+    chunks = [(g, c) for g in range(KV_LOCAL) for c in range(PER_GROUP // CHUNK)]
+    ready = {}
+
+    def after(g, c):
+        query_side(g, c)
+        if c == PER_GROUP // CHUNK - 1:
+            done = [ready[g, i] for i in range(c + 1)]
+            key_side(g, [x[0] for x in done], [x[1] for x in done])
+
+    for n in range(min(AHEAD, len(chunks))):
+        ready[chunks[n]] = products(*chunks[n])
+    for n, chunk in enumerate(chunks):
+        if n + AHEAD < len(chunks):
+            ready[chunks[n + AHEAD]] = products(*chunks[n + AHEAD])
+        if AHEAD == 0:
+            ready[chunk] = products(*chunk)
+        softmax(*chunk, *ready[chunk][2:])
+        if n >= BEHIND:
+            after(*chunks[n - BEHIND])
+    for chunk in chunks[len(chunks) - BEHIND :]:
+        after(*chunk)
+
+
+def attention(place, packing, lengths, plan, rows, prompt, slots):
     flops = 2 * 5 * KEYS * Q_WIDTH // HEAD * SLOTS * HEAD
     block = jax.ShapeDtypeStruct((LOCAL_ROWS, OUT_WIDTH), BF16)
     *back, grads = pl.pallas_call(
-        attention_kernel,
-        out_shape=(block,) * N_HEAD + (jax.ShapeDtypeStruct((PROMPT, 2 * KV_WIDTH), BF16),),
-        in_specs=[SMEM] * 3 + [VMEM] * (N_HEAD + 1),
+        functools.partial(attention_kernel, slots),
+        out_shape=(block,) * N_HEAD
+        + (jax.ShapeDtypeStruct((PLANE * slots, PIECE, 2 * KV_WIDTH), BF16),),
+        in_specs=[SMEM] * 4 + [VMEM] * (N_HEAD + 1),
         out_specs=(VMEM,) * (N_HEAD + 1),
         scratch_shapes=[
             pltpu.VMEM((KEYS, KV_WIDTH), BF16),
             pltpu.VMEM((KEYS, KV_WIDTH), BF16),
-            pltpu.VMEM((KEYS, PER_GROUP * SLOTS), BF16),
-            pltpu.VMEM((KEYS, PER_GROUP * SLOTS), BF16),
+            pltpu.VMEM((KV_LOCAL, KEYS, PER_GROUP * SLOTS), BF16),
+            pltpu.VMEM((KV_LOCAL, KEYS, PER_GROUP * SLOTS), BF16),
         ],
         compiler_params=params(32),
         cost_estimate=pl.CostEstimate(
             flops=flops, bytes_accessed=6 * 2**20, transcendentals=KEYS * SLOTS * 16
         ),
-    )(place, packing, lengths, *reversed(rows), prompt)
-    return back, grads
+    )(place, packing, lengths, plan, *reversed(rows), prompt)
+    return back, grads.reshape(PLANE, slots * PIECE, 2 * KV_WIDTH)
 
 
 def exchange(parts, axes):
@@ -399,17 +409,16 @@
         parts = exchange(select(plan, line, slots), plane)
         return collect(place, packing, plan, parts, slots)
 
-    def reduce(slots, grads):
-        parts = exchange(scatter(place, packing, plan, grads, slots), plane)
-        return sum_plane(plan, parts, slots)
+    def reduce(slots, prompt, *rows):
+        back, grads = attention(place, packing, lengths, plan, rows, prompt, slots)
+        return back, sum_plane(plan, exchange(grads, plane), slots)
 
     choice = plan[CHOICE, 0]
     prompt = lax.switch(
         choice, [functools.partial(gather, slots) for slots in SLOT_COUNTS], line
     )
-    back, grads = attention(place, packing, lengths, rows, prompt)
-    grads = lax.switch(
-        choice, [functools.partial(reduce, slots) for slots in SLOT_COUNTS], grads
+    back, grads = lax.switch(
+        choice, [functools.partial(reduce, slots) for slots in SLOT_COUNTS], prompt, *rows
     )
     grads = exchange(grads, "z")
     back = swap(back)

time: 97.5 us -> 92.5 us (0.949)
  blocking collectives: 27.6 us -> 24.7 us
  starting transfers between devices: 43.4 us -> 40.6 us
    all_to_all x2, blocking collectives: 27.6 us -> 24.7 us  [exchange(): return lax.all_to_all(parts, axes, split_axis=0, concat_axis=0, tiled=True)]
    all_to_all x2, starting transfers between devices: 25.2 us -> 22.4 us  [exchange(): return lax.all_to_all(parts, axes, split_axis=0, concat_axis=0, tiled=True)]
    pallas_call x2 -> x1, Pallas kernels: 4.57 us -> 3.73 us  [attention(): pl.pallas_call(functools.partial(attention_kernel, slots), out_shape=(blo...]
where the time goes in v5:
time: 92.5 us; the launch traced here: 91.7 us
  starting transfers between devices  40.6 us (44%)
  blocking collectives  24.7 us (27%)
  waiting for transfers between devices  12.9 us (14%)
  Pallas kernels  11.4 us (12%)
  between operations  1.42 us (2%)
    all_to_all x2, blocking collectives, exchange(): return lax.all_to_all(parts, axes, split_axis=0, concat_axis=0, tiled=True)  24.7 us
    all_to_all x2, starting transfers between devices, exchange(): return lax.all_to_all(parts, axes, split_axis=0, concat_axis=0, tiled=True)  22.4 us
    ppermute x6, starting transfers between devices, swap(): blocks[k] = lax.ppermute(blocks[k], ('xh', 'c'), pairs)  18.2 us
    all_to_all x2, waiting for transfers between devices, exchange(): return lax.all_to_all(parts, axes, split_axis=0, concat_axis=0, tiled=True)  9.69 us
    pallas_call x1, Pallas kernels, attention(): pl.pallas_call(functools.partial(attention_kernel, slots), out_shape=(blo...  3.73 us
    ppermute x6, waiting for transfers between devices, swap(): blocks[k] = lax.ppermute(blocks[k], ('xh', 'c'), pairs)  3.23 us
  transfers between devices with their start and end apart: 8, of which 3 were waited for; matrix products, arithmetic and copies ran while one was open for 1% of the time, Pallas kernels for 4%

profile of v5, /device:TPU:4, one launch (start us, length us, event | category | flops | bytes accessed | tf_op | source)
XLA Modules:
  0.0 91.7 jit_solution(9881475114452857284)
XLA Ops:
  0.6 1.6 %shard_map.95 = (bf16[32,4608]{1,0:T(8,128)(2,1)S(1)}, bf16[32,4608]{1,0:T(8,128)(2,1)S(1)}, bf16[32,4608]{1,0:T(8,128)(2,1)S(1)}, bf16[32,4608]{1,0:T(8,128)(2,1)S(1)}, bf16[16,16,512]{2,1,0:T(8,128)(2,1)}) custom-call(bf16[32,8192]{1,0:T(8,128)(2,1)} %q_ref.1, bf16[32,8192]{1,0:T(8,128)(2,1)} %g_ref.1, bf16[32,2,1024]{2,1,0:T(2,128)(2,1)} %kv_ref.1, ...), custom_call_target="tpu_custom_call" | custom-call | tf_op jit(solution)/shard_map/pallas_call | solution.py:151
  2.2 15.2 %all-to-all-start.12 = ((bf16[16,16,512]{2,1,0:T(8,128)(2,1)}), bf16[16,16,512]{2,1,0:T(8,128)(2,1)S(1)}, u32[]{:S(2)}, u32[]{:S(2)}) async-start(bf16[16,16,512]{2,1,0:T(8,128)(2,1)} %get-tuple-element.290), calls=%async_computation.12 | async-start | bytes 524288 | tf_op jit(solution)/shard_map/all_to_all | solution.py:388
  17.4 1.9 %collective-permute-start = (bf16[32,4608]{1,0:T(8,128)(2,1)S(1)}, bf16[32,4608]{1,0:T(8,128)(2,1)S(1)}, u32[]{:S(2)}, u32[]{:S(2)}) collective-permute-start(bf16[32,4608]{1,0:T(8,128)(2,1)S(1)} %get-tuple-element.286), channel_id=1, source_target_pairs={{0,3},{1,2},{2,1},{3,0},{4,7},{5,6},{6,5},{7,4},{8,11},{9,10},{10,... | collective-permute-start | bytes 884744 | tf_op jit(solution)/shard_map/ppermute | solution.py:395
  19.4 4.6 %collective-permute-start.1 = (bf16[32,4608]{1,0:T(8,128)(2,1)S(1)}, bf16[32,4608]{1,0:T(8,128)(2,1)S(1)}, u32[]{:S(2)}, u32[]{:S(2)}) collective-permute-start(bf16[32,4608]{1,0:T(8,128)(2,1)S(1)} %get-tuple-element.287), channel_id=1, source_target_pairs={{0,2},{1,3},{2,0},{3,1},{4,6},{5,7},{6,4},{7,5},{8,10},{9,11},{10,... | collective-permute-start | bytes 884744 | tf_op jit(solution)/shard_map/ppermute | solution.py:395
  23.9 2.6 %collective-permute-start.2 = (bf16[32,4608]{1,0:T(8,128)(2,1)S(1)}, bf16[32,4608]{1,0:T(8,128)(2,1)S(1)}, u32[]{:S(2)}, u32[]{:S(2)}) collective-permute-start(bf16[32,4608]{1,0:T(8,128)(2,1)S(1)} %get-tuple-element.288), channel_id=1, source_target_pairs={{0,1},{1,0},{2,3},{3,2},{4,5},{5,4},{6,7},{7,6},{8,9},{9,8},{10,11... | collective-permute-start | bytes 884744 | tf_op jit(solution)/shard_map/ppermute | solution.py:395
  26.5 0.1 pad_add_fusion.place_ref
  26.6 0.9 %shard_map.94 = s32[4,128]{1,0:T(4,128)S(1)} custom-call(s32[2]{0:T(128)S(1)} %pad_add_fusion.place_ref, s32[128]{0:T(128)} %packing_ref.1, s32[1,128]{1,0:T(1,128)} %bitcast.52), custom_call_target="tpu_custom_call" | custom-call | tf_op jit(solution)/shard_map/pallas_call | solution.py:88
  27.6 0.5 slice.3
  28.7 7.0 %all-to-all-done.12 = bf16[16,16,512]{2,1,0:T(8,128)(2,1)S(1)} async-done(((bf16[16,16,512]{2,1,0:T(8,128)(2,1)}), bf16[16,16,512]{2,1,0:T(8,128)(2,1)S(1)}, u32[]{:S(2)}, u32[]{:S(2)}) %all-to-all-start.12) | async-done | bytes 262176 | tf_op jit(solution)/shard_map/all_to_all | solution.py:388
  35.8 0.0 copy-start.5
  35.8 15.0 %conditional.2 = (bf16[256,512]{1,0:T(8,128)(2,1)S(1)}) conditional(s32[]{:T(128)} %bitcast.27, (s32[4,128]{1,0:T(4,128)S(1)}, bf16[16,16,512]{2,1,0:T(8,128)(2,1)S(1)}, s32[2]{0:T(128)S(1)}, s32[128]{0:T(128)}) %tuple.50, (s32[4,128]{1,0:T(4,128)S(1)}, bf16[16,16,512]{2,1,0:T(8,128)(2,1)S(1)}, s32[2]{0:T(128)S(1)}, ...), branch_computations={%region_0.0_spmd, %region_1.0_spmd, %region_2.0_spmd, %region_3.0_... | conditional | bytes 4196388 | solution.py:417
  35.8 0.8 branch_0_fun.4
  36.6 13.5 %all_to_all.58 = bf16[8,64,512]{2,1,0:T(8,128)(2,1)S(1)} all-to-all(bf16[8,64,512]{2,1,0:T(8,128)(2,1)S(1)} %bitcast.46), channel_id=1, replica_groups=mesh['xl'=2,'z'=16,'y'=4,'xh'=2,'c'=2] {'xl','y'}, dimensions={0} | all-to-all | bytes 1048576 | tf_op jit(solution)/shard_map/cond/branch_0_fun/all_to_all | solution.py:388
  50.1 0.7 branch_0_fun.5
  50.8 0.0 collective-permute-done
  50.8 0.0 collective-permute-done.1
  50.8 0.0 collective-permute-done.2
  50.8 0.0 copy-done.5
  50.8 16.5 %conditional.3 = (bf16[32,2560]{1,0:T(8,128)(2,1)S(1)}, bf16[32,2560]{1,0:T(8,128)(2,1)S(1)}, bf16[32,2560]{1,0:T(8,128)(2,1)S(1)}, bf16[32,2560]{1,0:T(8,128)(2,1)S(1)}, bf16[16,16,512]{2,1,0:T(8,128)(2,1)}) conditional(s32[]{:T(128)} %bitcast.27, (s32[2]{0:T(128)S(1)}, s32[128]{0:T(128)}, s32[128]{0:T(128)S(1)}, ...), branch_computations={%region_6.0_spmd, %region_7.0_spmd, %region_8.0_spmd, %region_9.0_... | conditional | flops 1006632960 | bytes 10485800 | solution.py:420
  50.9 3.7 %branch_0_fun.6 = (bf16[32,2560]{1,0:T(8,128)(2,1)S(1)}, bf16[32,2560]{1,0:T(8,128)(2,1)S(1)}, bf16[32,2560]{1,0:T(8,128)(2,1)S(1)}, bf16[32,2560]{1,0:T(8,128)(2,1)S(1)}, bf16[32,16,512]{2,1,0:T(8,128)(2,1)S(1)}) custom-call(s32[2]{0:T(128)S(1)} %get-tuple-element.187.place_ref, s32[128]{0:T(128)} %get-tuple-element.188.packing_ref, ...), custom_call_target="tpu_custom_call" | custom-call | flops 1006632960 | bytes 6291456 | tf_op jit(solution)/shard_map/cond/branch_0_fun/pallas_call | solution.py:367
  54.6 11.2 %all_to_all.64 = bf16[8,64,512]{2,1,0:T(8,128)(2,1)S(1)} all-to-all(bf16[8,64,512]{2,1,0:T(8,128)(2,1)S(1)} %bitcast.51), channel_id=1, replica_groups=mesh['xl'=2,'z'=16,'y'=4,'xh'=2,'c'=2] {'xl','y'}, dimensions={0} | all-to-all | bytes 1048576 | tf_op jit(solution)/shard_map/cond/branch_0_fun/all_to_all | solution.py:388
  65.8 1.6 %branch_0_fun.7 = bf16[16,16,512]{2,1,0:T(8,128)(2,1)} custom-call(s32[4,128]{1,0:T(4,128)S(1)} %get-tuple-element.190.plan_ref, bf16[32,16,512]{2,1,0:T(8,128)(2,1)S(1)} %bitcast.45), custom_call_target="tpu_custom_call" | custom-call | tf_op jit(solution)/shard_map/cond/branch_0_fun/pallas_call | solution.py:225
  67.4 7.2 %all-to-all-start.13 = ((bf16[16,16,512]{2,1,0:T(8,128)(2,1)}), bf16[16,16,512]{2,1,0:T(8,128)(2,1)S(1)}, u32[]{:S(2)}, u32[]{:S(2)}) async-start(bf16[16,16,512]{2,1,0:T(8,128)(2,1)} %get-tuple-element.297), calls=%async_computation.13 | async-start | bytes 524288 | tf_op jit(solution)/shard_map/all_to_all | solution.py:388
  74.6 1.9 %collective-permute-start.3 = (bf16[32,2560]{1,0:T(8,128)(2,1)S(1)}, bf16[32,2560]{1,0:T(8,128)(2,1)S(1)}, u32[]{:S(2)}, u32[]{:S(2)}) collective-permute-start(bf16[32,2560]{1,0:T(8,128)(2,1)S(1)} %get-tuple-element.291), channel_id=1, source_target_pairs={{0,3},{1,2},{2,1},{3,0},{4,7},{5,6},{6,5},{7,4},{8,11},{9,10},{10,... | collective-permute-start | bytes 491528 | tf_op jit(solution)/shard_map/ppermute | solution.py:395
  76.6 2.7 %collective-permute-start.4 = (bf16[32,2560]{1,0:T(8,128)(2,1)S(1)}, bf16[32,2560]{1,0:T(8,128)(2,1)S(1)}, u32[]{:S(2)}, u32[]{:S(2)}) collective-permute-start(bf16[32,2560]{1,0:T(8,128)(2,1)S(1)} %get-tuple-element.292), channel_id=1, source_target_pairs={{0,2},{1,3},{2,0},{3,1},{4,6},{5,7},{6,4},{7,5},{8,10},{9,11},{10,... | collective-permute-start | bytes 491528 | tf_op jit(solution)/shard_map/ppermute | solution.py:395
  79.3 4.5 %collective-permute-start.5 = (bf16[32,2560]{1,0:T(8,128)(2,1)S(1)}, bf16[32,2560]{1,0:T(8,128)(2,1)S(1)}, u32[]{:S(2)}, u32[]{:S(2)}) collective-permute-start(bf16[32,2560]{1,0:T(8,128)(2,1)S(1)} %get-tuple-element.293), channel_id=1, source_target_pairs={{0,1},{1,0},{2,3},{3,2},{4,5},{5,4},{6,7},{7,6},{8,9},{9,8},{10,11... | collective-permute-start | bytes 491528 | tf_op jit(solution)/shard_map/ppermute | solution.py:395
  83.7 0.0 collective-permute-done.3.refs_0_
  83.7 3.2 %collective-permute-done.4.refs_1_ = bf16[32,2560]{1,0:T(8,128)(2,1)S(1)} collective-permute-done((bf16[32,2560]{1,0:T(8,128)(2,1)S(1)}, bf16[32,2560]{1,0:T(8,128)(2,1)S(1)}, u32[]{:S(2)}, u32[]{:S(2)}) %collective-permute-start.4) | collective-permute-done | bytes 163872 | tf_op jit(solution)/shard_map/ppermute | solution.py:395
  87.0 0.0 collective-permute-done.5.refs_2_
  87.0 1.4 %shard_map.96 = (bf16[32,8192]{1,0:T(8,128)(2,1)}, bf16[32,2,1024]{2,1,0:T(2,128)(2,1)}) custom-call(s32[2]{0:T(128)S(1)} %pad_add_fusion.place_ref, bf16[32,2560]{1,0:T(8,128)(2,1)S(1)} %collective-permute-done.3.refs_0_, bf16[32,2560]{1,0:T(8,128)(2,1)S(1)} %collective-permute-done.4.refs_1_, bf16[32,2560]{1,0:T(8,128)(2,1)S(1)} %collective-permute-done.5.refs_2_, ...), custom_call_target="tpu_custom_call" | custom-call | tf_op jit(solution)/shard_map/pallas_call | solution.py:178
  88.4 2.7 %all-to-all-done.13.in_ref = bf16[16,16,512]{2,1,0:T(8,128)(2,1)S(1)} async-done(((bf16[16,16,512]{2,1,0:T(8,128)(2,1)}), bf16[16,16,512]{2,1,0:T(8,128)(2,1)S(1)}, u32[]{:S(2)}, u32[]{:S(2)}) %all-to-all-start.13) | async-done | bytes 262176 | tf_op jit(solution)/shard_map/all_to_all | solution.py:388
  91.1 0.7 shard_map.97
Async XLA Ops:
  2.2 33.6 %all-to-all-start.12 = ((bf16[16,16,512]{2,1,0:T(8,128)(2,1)}), bf16[16,16,512]{2,1,0:T(8,128)(2,1)S(1)}, u32[]{:S(2)}, u32[]{:S(2)}) async-start(bf16[16,16,512]{2,1,0:T(8,128)(2,1)} %get-tuple-element.290), calls=%async_computation.12 | async-start | bytes 524288 | tf_op jit(solution)/shard_map/all_to_all | solution.py:388
  17.4 33.4 %collective-permute-start = (bf16[32,4608]{1,0:T(8,128)(2,1)S(1)}, bf16[32,4608]{1,0:T(8,128)(2,1)S(1)}, u32[]{:S(2)}, u32[]{:S(2)}) collective-permute-start(bf16[32,4608]{1,0:T(8,128)(2,1)S(1)} %get-tuple-element.286), channel_id=1, source_target_pairs={{0,3},{1,2},{2,1},{3,0},{4,7},{5,6},{6,5},{7,4},{8,11},{9,10},{10,... | collective-permute-start | bytes 884744 | tf_op jit(solution)/shard_map/ppermute | solution.py:395
  19.4 31.5 %collective-permute-start.1 = (bf16[32,4608]{1,0:T(8,128)(2,1)S(1)}, bf16[32,4608]{1,0:T(8,128)(2,1)S(1)}, u32[]{:S(2)}, u32[]{:S(2)}) collective-permute-start(bf16[32,4608]{1,0:T(8,128)(2,1)S(1)} %get-tuple-element.287), channel_id=1, source_target_pairs={{0,2},{1,3},{2,0},{3,1},{4,6},{5,7},{6,4},{7,5},{8,10},{9,11},{10,... | collective-permute-start | bytes 884744 | tf_op jit(solution)/shard_map/ppermute | solution.py:395
  23.9 26.9 %collective-permute-start.2 = (bf16[32,4608]{1,0:T(8,128)(2,1)S(1)}, bf16[32,4608]{1,0:T(8,128)(2,1)S(1)}, u32[]{:S(2)}, u32[]{:S(2)}) collective-permute-start(bf16[32,4608]{1,0:T(8,128)(2,1)S(1)} %get-tuple-element.288), channel_id=1, source_target_pairs={{0,1},{1,0},{2,3},{3,2},{4,5},{5,4},{6,7},{7,6},{8,9},{9,8},{10,11... | collective-permute-start | bytes 884744 | tf_op jit(solution)/shard_map/ppermute | solution.py:395
  35.8 15.0 %copy-start.5 = (s32[128]{0:T(128)S(1)}, s32[128]{0:T(128)}, u32[]{:S(2)}) copy-start(s32[128]{0:T(128)} %param.24) | copy-start | bytes 1540
  67.4 23.7 %all-to-all-start.13 = ((bf16[16,16,512]{2,1,0:T(8,128)(2,1)}), bf16[16,16,512]{2,1,0:T(8,128)(2,1)S(1)}, u32[]{:S(2)}, u32[]{:S(2)}) async-start(bf16[16,16,512]{2,1,0:T(8,128)(2,1)} %get-tuple-element.297), calls=%async_computation.13 | async-start | bytes 524288 | tf_op jit(solution)/shard_map/all_to_all | solution.py:388
  74.6 9.1 %collective-permute-start.3 = (bf16[32,2560]{1,0:T(8,128)(2,1)S(1)}, bf16[32,2560]{1,0:T(8,128)(2,1)S(1)}, u32[]{:S(2)}, u32[]{:S(2)}) collective-permute-start(bf16[32,2560]{1,0:T(8,128)(2,1)S(1)} %get-tuple-element.291), channel_id=1, source_target_pairs={{0,3},{1,2},{2,1},{3,0},{4,7},{5,6},{6,5},{7,4},{8,11},{9,10},{10,... | collective-permute-start | bytes 491528 | tf_op jit(solution)/shard_map/ppermute | solution.py:395
  76.6 10.4 %collective-permute-start.4 = (bf16[32,2560]{1,0:T(8,128)(2,1)S(1)}, bf16[32,2560]{1,0:T(8,128)(2,1)S(1)}, u32[]{:S(2)}, u32[]{:S(2)}) collective-permute-start(bf16[32,2560]{1,0:T(8,128)(2,1)S(1)} %get-tuple-element.292), channel_id=1, source_target_pairs={{0,2},{1,3},{2,0},{3,1},{4,6},{5,7},{6,4},{7,5},{8,10},{9,11},{10,... | collective-permute-start | bytes 491528 | tf_op jit(solution)/shard_map/ppermute | solution.py:395
  79.3 7.7 %collective-permute-start.5 = (bf16[32,2560]{1,0:T(8,128)(2,1)S(1)}, bf16[32,2560]{1,0:T(8,128)(2,1)S(1)}, u32[]{:S(2)}, u32[]{:S(2)}) collective-permute-start(bf16[32,2560]{1,0:T(8,128)(2,1)S(1)} %get-tuple-element.293), channel_id=1, source_target_pairs={{0,1},{1,0},{2,3},{3,2},{4,5},{5,4},{6,7},{7,6},{8,9},{9,8},{10,11... | collective-permute-start | bytes 491528 | tf_op jit(solution)/shard_map/ppermute | solution.py:395

commit v6 on v5

--- a/solution.py
+++ b/solution.py
@@ -95,9 +95,7 @@
 
 def select_kernel(slots, plan_ref, line_ref, out_ref):
     for d in range(PLANE):
-
-        @pl.loop(0, plan_ref[COUNT, d * GROUP])
-        def _(c, d=d):
+        for c in range(slots):
             out_ref[d * slots + c] = line_ref[plan_ref[SOURCE, d * GROUP + c]]
 
 

time: 92.5 us -> 95.4 us (1.031)
  blocking collectives: 24.7 us -> 26.2 us
  starting transfers between devices: 40.6 us -> 42.1 us
    all_to_all x2, starting transfers between devices: 22.4 us -> 24 us  [exchange(): return lax.all_to_all(parts, axes, split_axis=0, concat_axis=0, tiled=True)]
    all_to_all x2, blocking collectives: 24.7 us -> 26.2 us  [exchange(): return lax.all_to_all(parts, axes, split_axis=0, concat_axis=0, tiled=True)]
where the time goes in v6:
time: 95.4 us; the launch traced here: 94.7 us
  starting transfers between devices  42.1 us (44%)
  blocking collectives  26.2 us (27%)
  waiting for transfers between devices  13 us (14%)
  Pallas kernels  11.2 us (12%)
  between operations  1.42 us (1%)
    all_to_all x2, blocking collectives, exchange(): return lax.all_to_all(parts, axes, split_axis=0, concat_axis=0, tiled=True)  26.2 us
    all_to_all x2, starting transfers between devices, exchange(): return lax.all_to_all(parts, axes, split_axis=0, concat_axis=0, tiled=True)  24 us
    ppermute x6, starting transfers between devices, swap(): blocks[k] = lax.ppermute(blocks[k], ('xh', 'c'), pairs)  18.2 us
    all_to_all x2, waiting for transfers between devices, exchange(): return lax.all_to_all(parts, axes, split_axis=0, concat_axis=0, tiled=True)  9.82 us
    pallas_call x1, Pallas kernels, attention(): pl.pallas_call(functools.partial(attention_kernel, slots), out_shape=(blo...  3.72 us
    ppermute x6, waiting for transfers between devices, swap(): blocks[k] = lax.ppermute(blocks[k], ('xh', 'c'), pairs)  3.22 us
  transfers between devices with their start and end apart: 8, of which 3 were waited for; matrix products, arithmetic and copies ran while one was open for 1% of the time, Pallas kernels for 4%

profile of v6, /device:TPU:4, one launch (start us, length us, event | category | flops | bytes accessed | tf_op | source)
XLA Modules:
  0.0 94.7 jit_solution(16168735469163556155)
XLA Ops:
  0.6 1.6 %shard_map.95 = (bf16[32,4608]{1,0:T(8,128)(2,1)S(1)}, bf16[32,4608]{1,0:T(8,128)(2,1)S(1)}, bf16[32,4608]{1,0:T(8,128)(2,1)S(1)}, bf16[32,4608]{1,0:T(8,128)(2,1)S(1)}, bf16[16,16,512]{2,1,0:T(8,128)(2,1)}) custom-call(bf16[32,8192]{1,0:T(8,128)(2,1)} %q_ref.1, bf16[32,8192]{1,0:T(8,128)(2,1)} %g_ref.1, bf16[32,2,1024]{2,1,0:T(2,128)(2,1)} %kv_ref.1, ...), custom_call_target="tpu_custom_call" | custom-call | tf_op jit(solution)/shard_map/pallas_call | solution.py:149
  2.2 15.2 %all-to-all-start.12 = ((bf16[16,16,512]{2,1,0:T(8,128)(2,1)}), bf16[16,16,512]{2,1,0:T(8,128)(2,1)S(1)}, u32[]{:S(2)}, u32[]{:S(2)}) async-start(bf16[16,16,512]{2,1,0:T(8,128)(2,1)} %get-tuple-element.290), calls=%async_computation.12 | async-start | bytes 524288 | tf_op jit(solution)/shard_map/all_to_all | solution.py:386
  17.4 1.9 %collective-permute-start = (bf16[32,4608]{1,0:T(8,128)(2,1)S(1)}, bf16[32,4608]{1,0:T(8,128)(2,1)S(1)}, u32[]{:S(2)}, u32[]{:S(2)}) collective-permute-start(bf16[32,4608]{1,0:T(8,128)(2,1)S(1)} %get-tuple-element.286), channel_id=1, source_target_pairs={{0,3},{1,2},{2,1},{3,0},{4,7},{5,6},{6,5},{7,4},{8,11},{9,10},{10,... | collective-permute-start | bytes 884744 | tf_op jit(solution)/shard_map/ppermute | solution.py:393
  19.4 4.6 %collective-permute-start.1 = (bf16[32,4608]{1,0:T(8,128)(2,1)S(1)}, bf16[32,4608]{1,0:T(8,128)(2,1)S(1)}, u32[]{:S(2)}, u32[]{:S(2)}) collective-permute-start(bf16[32,4608]{1,0:T(8,128)(2,1)S(1)} %get-tuple-element.287), channel_id=1, source_target_pairs={{0,2},{1,3},{2,0},{3,1},{4,6},{5,7},{6,4},{7,5},{8,10},{9,11},{10,... | collective-permute-start | bytes 884744 | tf_op jit(solution)/shard_map/ppermute | solution.py:393
  23.9 2.6 %collective-permute-start.2 = (bf16[32,4608]{1,0:T(8,128)(2,1)S(1)}, bf16[32,4608]{1,0:T(8,128)(2,1)S(1)}, u32[]{:S(2)}, u32[]{:S(2)}) collective-permute-start(bf16[32,4608]{1,0:T(8,128)(2,1)S(1)} %get-tuple-element.288), channel_id=1, source_target_pairs={{0,1},{1,0},{2,3},{3,2},{4,5},{5,4},{6,7},{7,6},{8,9},{9,8},{10,11... | collective-permute-start | bytes 884744 | tf_op jit(solution)/shard_map/ppermute | solution.py:393
  26.5 0.1 pad_add_fusion.place_ref
  26.6 0.9 %shard_map.94 = s32[4,128]{1,0:T(4,128)S(1)} custom-call(s32[2]{0:T(128)S(1)} %pad_add_fusion.place_ref, s32[128]{0:T(128)} %packing_ref.1, s32[1,128]{1,0:T(1,128)} %bitcast.52), custom_call_target="tpu_custom_call" | custom-call | tf_op jit(solution)/shard_map/pallas_call | solution.py:88
  27.6 0.5 slice.3
  28.7 7.0 %all-to-all-done.12 = bf16[16,16,512]{2,1,0:T(8,128)(2,1)S(1)} async-done(((bf16[16,16,512]{2,1,0:T(8,128)(2,1)}), bf16[16,16,512]{2,1,0:T(8,128)(2,1)S(1)}, u32[]{:S(2)}, u32[]{:S(2)}) %all-to-all-start.12) | async-done | bytes 262176 | tf_op jit(solution)/shard_map/all_to_all | solution.py:386
  35.8 0.0 copy-start.5
  35.8 15.6 %conditional.2 = (bf16[256,512]{1,0:T(8,128)(2,1)S(1)}) conditional(s32[]{:T(128)} %bitcast.27, (s32[4,128]{1,0:T(4,128)S(1)}, bf16[16,16,512]{2,1,0:T(8,128)(2,1)S(1)}, s32[2]{0:T(128)S(1)}, s32[128]{0:T(128)}) %tuple.50, (s32[4,128]{1,0:T(4,128)S(1)}, bf16[16,16,512]{2,1,0:T(8,128)(2,1)S(1)}, s32[2]{0:T(128)S(1)}, ...), branch_computations={%region_0.0_spmd, %region_1.0_spmd, %region_2.0_spmd, %region_3.0_... | conditional | bytes 4196388 | solution.py:415
  35.8 0.0 copy-start
  35.8 0.6 branch_1_fun.4
  36.4 14.3 %all_to_all.59 = bf16[8,80,512]{2,1,0:T(8,128)(2,1)S(1)} all-to-all(bf16[8,80,512]{2,1,0:T(8,128)(2,1)S(1)} %bitcast.42), channel_id=1, replica_groups=mesh['xl'=2,'z'=16,'y'=4,'xh'=2,'c'=2] {'xl','y'}, dimensions={0} | all-to-all | bytes 1310720 | tf_op jit(solution)/shard_map/cond/branch_1_fun/all_to_all | solution.py:386
  50.7 0.0 copy-done
  50.7 0.6 branch_1_fun.5
  51.3 0.0 collective-permute-done
  51.4 0.0 collective-permute-done.1
  51.4 0.0 collective-permute-done.2
  51.4 0.0 copy-done.5
  51.4 17.3 %conditional.3 = (bf16[32,2560]{1,0:T(8,128)(2,1)S(1)}, bf16[32,2560]{1,0:T(8,128)(2,1)S(1)}, bf16[32,2560]{1,0:T(8,128)(2,1)S(1)}, bf16[32,2560]{1,0:T(8,128)(2,1)S(1)}, bf16[16,16,512]{2,1,0:T(8,128)(2,1)}) conditional(s32[]{:T(128)} %bitcast.27, (s32[2]{0:T(128)S(1)}, s32[128]{0:T(128)}, s32[128]{0:T(128)S(1)}, ...), branch_computations={%region_6.0_spmd, %region_7.0_spmd, %region_8.0_spmd, %region_9.0_... | conditional | flops 1006632960 | bytes 10485800 | solution.py:418
  51.4 3.7 %branch_1_fun.6 = (bf16[32,2560]{1,0:T(8,128)(2,1)S(1)}, bf16[32,2560]{1,0:T(8,128)(2,1)S(1)}, bf16[32,2560]{1,0:T(8,128)(2,1)S(1)}, bf16[32,2560]{1,0:T(8,128)(2,1)S(1)}, bf16[40,16,512]{2,1,0:T(8,128)(2,1)S(1)}) custom-call(s32[2]{0:T(128)S(1)} %get-tuple-element.201.place_ref, s32[128]{0:T(128)} %get-tuple-element.202.packing_ref, ...), custom_call_target="tpu_custom_call" | custom-call | flops 1006632960 | bytes 6291456 | tf_op jit(solution)/shard_map/cond/branch_1_fun/pallas_call | solution.py:365
  55.2 11.9 %all_to_all.65 = bf16[8,80,512]{2,1,0:T(8,128)(2,1)S(1)} all-to-all(bf16[8,80,512]{2,1,0:T(8,128)(2,1)S(1)} %bitcast.50), channel_id=1, replica_groups=mesh['xl'=2,'z'=16,'y'=4,'xh'=2,'c'=2] {'xl','y'}, dimensions={0} | all-to-all | bytes 1310720 | tf_op jit(solution)/shard_map/cond/branch_1_fun/all_to_all | solution.py:386
  67.1 1.6 %branch_1_fun.7 = bf16[16,16,512]{2,1,0:T(8,128)(2,1)} custom-call(s32[4,128]{1,0:T(4,128)S(1)} %get-tuple-element.204.plan_ref, bf16[40,16,512]{2,1,0:T(8,128)(2,1)S(1)} %bitcast.41), custom_call_target="tpu_custom_call" | custom-call | tf_op jit(solution)/shard_map/cond/branch_1_fun/pallas_call | solution.py:223
  68.7 8.8 %all-to-all-start.13 = ((bf16[16,16,512]{2,1,0:T(8,128)(2,1)}), bf16[16,16,512]{2,1,0:T(8,128)(2,1)S(1)}, u32[]{:S(2)}, u32[]{:S(2)}) async-start(bf16[16,16,512]{2,1,0:T(8,128)(2,1)} %get-tuple-element.297), calls=%async_computation.13 | async-start | bytes 524288 | tf_op jit(solution)/shard_map/all_to_all | solution.py:386
  77.4 1.9 %collective-permute-start.3 = (bf16[32,2560]{1,0:T(8,128)(2,1)S(1)}, bf16[32,2560]{1,0:T(8,128)(2,1)S(1)}, u32[]{:S(2)}, u32[]{:S(2)}) collective-permute-start(bf16[32,2560]{1,0:T(8,128)(2,1)S(1)} %get-tuple-element.291), channel_id=1, source_target_pairs={{0,3},{1,2},{2,1},{3,0},{4,7},{5,6},{6,5},{7,4},{8,11},{9,10},{10,... | collective-permute-start | bytes 491528 | tf_op jit(solution)/shard_map/ppermute | solution.py:393
  79.4 2.7 %collective-permute-start.4 = (bf16[32,2560]{1,0:T(8,128)(2,1)S(1)}, bf16[32,2560]{1,0:T(8,128)(2,1)S(1)}, u32[]{:S(2)}, u32[]{:S(2)}) collective-permute-start(bf16[32,2560]{1,0:T(8,128)(2,1)S(1)} %get-tuple-element.292), channel_id=1, source_target_pairs={{0,2},{1,3},{2,0},{3,1},{4,6},{5,7},{6,4},{7,5},{8,10},{9,11},{10,... | collective-permute-start | bytes 491528 | tf_op jit(solution)/shard_map/ppermute | solution.py:393
  82.1 4.5 %collective-permute-start.5 = (bf16[32,2560]{1,0:T(8,128)(2,1)S(1)}, bf16[32,2560]{1,0:T(8,128)(2,1)S(1)}, u32[]{:S(2)}, u32[]{:S(2)}) collective-permute-start(bf16[32,2560]{1,0:T(8,128)(2,1)S(1)} %get-tuple-element.293), channel_id=1, source_target_pairs={{0,1},{1,0},{2,3},{3,2},{4,5},{5,4},{6,7},{7,6},{8,9},{9,8},{10,11... | collective-permute-start | bytes 491528 | tf_op jit(solution)/shard_map/ppermute | solution.py:393
  86.5 0.0 collective-permute-done.3.refs_0_
  86.6 3.2 %collective-permute-done.4.refs_1_ = bf16[32,2560]{1,0:T(8,128)(2,1)S(1)} collective-permute-done((bf16[32,2560]{1,0:T(8,128)(2,1)S(1)}, bf16[32,2560]{1,0:T(8,128)(2,1)S(1)}, u32[]{:S(2)}, u32[]{:S(2)}) %collective-permute-start.4) | collective-permute-done | bytes 163872 | tf_op jit(solution)/shard_map/ppermute | solution.py:393
  89.8 0.0 collective-permute-done.5.refs_2_
  89.8 1.4 %shard_map.96 = (bf16[32,8192]{1,0:T(8,128)(2,1)}, bf16[32,2,1024]{2,1,0:T(2,128)(2,1)}) custom-call(s32[2]{0:T(128)S(1)} %pad_add_fusion.place_ref, bf16[32,2560]{1,0:T(8,128)(2,1)S(1)} %collective-permute-done.3.refs_0_, bf16[32,2560]{1,0:T(8,128)(2,1)S(1)} %collective-permute-done.4.refs_1_, bf16[32,2560]{1,0:T(8,128)(2,1)S(1)} %collective-permute-done.5.refs_2_, ...), custom_call_target="tpu_custom_call" | custom-call | tf_op jit(solution)/shard_map/pallas_call | solution.py:176
  91.2 2.8 %all-to-all-done.13.in_ref = bf16[16,16,512]{2,1,0:T(8,128)(2,1)S(1)} async-done(((bf16[16,16,512]{2,1,0:T(8,128)(2,1)}), bf16[16,16,512]{2,1,0:T(8,128)(2,1)S(1)}, u32[]{:S(2)}, u32[]{:S(2)}) %all-to-all-start.13) | async-done | bytes 262176 | tf_op jit(solution)/shard_map/all_to_all | solution.py:386
  94.0 0.7 shard_map.97
Async XLA Ops:
  2.2 33.6 %all-to-all-start.12 = ((bf16[16,16,512]{2,1,0:T(8,128)(2,1)}), bf16[16,16,512]{2,1,0:T(8,128)(2,1)S(1)}, u32[]{:S(2)}, u32[]{:S(2)}) async-start(bf16[16,16,512]{2,1,0:T(8,128)(2,1)} %get-tuple-element.290), calls=%async_computation.12 | async-start | bytes 524288 | tf_op jit(solution)/shard_map/all_to_all | solution.py:386
  17.4 33.9 %collective-permute-start = (bf16[32,4608]{1,0:T(8,128)(2,1)S(1)}, bf16[32,4608]{1,0:T(8,128)(2,1)S(1)}, u32[]{:S(2)}, u32[]{:S(2)}) collective-permute-start(bf16[32,4608]{1,0:T(8,128)(2,1)S(1)} %get-tuple-element.286), channel_id=1, source_target_pairs={{0,3},{1,2},{2,1},{3,0},{4,7},{5,6},{6,5},{7,4},{8,11},{9,10},{10,... | collective-permute-start | bytes 884744 | tf_op jit(solution)/shard_map/ppermute | solution.py:393
  19.4 32.0 %collective-permute-start.1 = (bf16[32,4608]{1,0:T(8,128)(2,1)S(1)}, bf16[32,4608]{1,0:T(8,128)(2,1)S(1)}, u32[]{:S(2)}, u32[]{:S(2)}) collective-permute-start(bf16[32,4608]{1,0:T(8,128)(2,1)S(1)} %get-tuple-element.287), channel_id=1, source_target_pairs={{0,2},{1,3},{2,0},{3,1},{4,6},{5,7},{6,4},{7,5},{8,10},{9,11},{10,... | collective-permute-start | bytes 884744 | tf_op jit(solution)/shard_map/ppermute | solution.py:393
  23.9 27.4 %collective-permute-start.2 = (bf16[32,4608]{1,0:T(8,128)(2,1)S(1)}, bf16[32,4608]{1,0:T(8,128)(2,1)S(1)}, u32[]{:S(2)}, u32[]{:S(2)}) collective-permute-start(bf16[32,4608]{1,0:T(8,128)(2,1)S(1)} %get-tuple-element.288), channel_id=1, source_target_pairs={{0,1},{1,0},{2,3},{3,2},{4,5},{5,4},{6,7},{7,6},{8,9},{9,8},{10,11... | collective-permute-start | bytes 884744 | tf_op jit(solution)/shard_map/ppermute | solution.py:393
  35.8 15.6 %copy-start.5 = (s32[128]{0:T(128)S(1)}, s32[128]{0:T(128)}, u32[]{:S(2)}) copy-start(s32[128]{0:T(128)} %param.24) | copy-start | bytes 1540
  35.8 14.9 %copy-start = (s32[128]{0:T(128)S(1)}, s32[128]{0:T(128)}, u32[]{:S(2)}) copy-start(s32[128]{0:T(128)} %get-tuple-element.168.packing_ref) | copy-start | bytes 1540 | tf_op jit(solution)/shard_map/cond
  68.7 25.3 %all-to-all-start.13 = ((bf16[16,16,512]{2,1,0:T(8,128)(2,1)}), bf16[16,16,512]{2,1,0:T(8,128)(2,1)S(1)}, u32[]{:S(2)}, u32[]{:S(2)}) async-start(bf16[16,16,512]{2,1,0:T(8,128)(2,1)} %get-tuple-element.297), calls=%async_computation.13 | async-start | bytes 524288 | tf_op jit(solution)/shard_map/all_to_all | solution.py:386
  77.4 9.1 %collective-permute-start.3 = (bf16[32,2560]{1,0:T(8,128)(2,1)S(1)}, bf16[32,2560]{1,0:T(8,128)(2,1)S(1)}, u32[]{:S(2)}, u32[]{:S(2)}) collective-permute-start(bf16[32,2560]{1,0:T(8,128)(2,1)S(1)} %get-tuple-element.291), channel_id=1, source_target_pairs={{0,3},{1,2},{2,1},{3,0},{4,7},{5,6},{6,5},{7,4},{8,11},{9,10},{10,... | collective-permute-start | bytes 491528 | tf_op jit(solution)/shard_map/ppermute | solution.py:393
  79.4 10.4 %collective-permute-start.4 = (bf16[32,2560]{1,0:T(8,128)(2,1)S(1)}, bf16[32,2560]{1,0:T(8,128)(2,1)S(1)}, u32[]{:S(2)}, u32[]{:S(2)}) collective-permute-start(bf16[32,2560]{1,0:T(8,128)(2,1)S(1)} %get-tuple-element.292), channel_id=1, source_target_pairs={{0,2},{1,3},{2,0},{3,1},{4,6},{5,7},{6,4},{7,5},{8,10},{9,11},{10,... | collective-permute-start | bytes 491528 | tf_op jit(solution)/shard_map/ppermute | solution.py:393
  82.1 7.7 %collective-permute-start.5 = (bf16[32,2560]{1,0:T(8,128)(2,1)S(1)}, bf16[32,2560]{1,0:T(8,128)(2,1)S(1)}, u32[]{:S(2)}, u32[]{:S(2)}) collective-permute-start(bf16[32,2560]{1,0:T(8,128)(2,1)S(1)} %get-tuple-element.293), channel_id=1, source_target_pairs={{0,1},{1,0},{2,3},{3,2},{4,5},{5,4},{6,7},{7,6},{8,9},{9,8},{10,11... | collective-permute-start | bytes 491528 | tf_op jit(solution)/shard_map/ppermute | solution.py:393
